TPU v7x, 512 devices: a whole 4x4x16 slice. The times are simulated.
512 devices in a mesh: slab: 64 (over z_lo, x, core), head: 8 (over y, z_hi).
Axes of the slice: x: 4, y: 4, z: 16 (z_hi: 2, z_lo: 8; z = z_hi * 8 + z_lo), core: 2. Of those that a mesh axis runs over, the one named last changes fastest.
Arguments:
- tokens: bfloat16 [64, 64, 16, 768], P('slab', 'head'), may hold values from -60 to 60
- cotangent: bfloat16 [64, 64, 16, 768], P('slab', 'head'), may hold values from -16 to 16
- weights: bfloat16 [768, 4, 512], P('slab', None, 'head'), may hold values from -2 to 2
- norm_gain: float32 [768], replicated, may hold values from 0.5 to 1.5
- norm_bias: float32 [768], replicated, may hold values from -3 to 3
Outputs:
- grad_tokens: bfloat16 [64, 64, 16, 768], P('slab', 'head')
- grad_weights: float32 [768, 4, 512], P('slab', None, 'head')
- grad_norm: float32 [2, 768], replicated
All inputs are finite; a program needn't handle non-finite values.
Results may differ from a plain program's by a relative error of at most 0.011.
Values may be sent and summed in bfloat16 or wider, within the bound.
A program may use at most 64 MiB of HBM per device.

v0:
```python
import jax
import jax.numpy as jnp
from jax import lax
from jax.sharding import PartitionSpec as P

HD = 64


def line_grads(q_lines, k_lines, v_lines, u_lines):
    score_scale = 1.0 / q_lines.shape[-1] ** 0.5
    scores = (
        jnp.einsum("blgd,bmgd->bglm", q_lines, k_lines, preferred_element_type=jnp.float32)
        * score_scale
    )
    probs_f = jax.nn.softmax(scores, axis=-1)
    probs_low = probs_f.astype(jnp.bfloat16)
    output = jnp.einsum(
        "bglm,bmgd->blgd", probs_low, v_lines, preferred_element_type=jnp.float32
    ).astype(jnp.bfloat16)
    dprobs = jnp.einsum("blgd,bmgd->bglm", u_lines, v_lines, preferred_element_type=jnp.float32)
    delta = jnp.sum(probs_f * dprobs, axis=-1, keepdims=True)
    dscores = (probs_f * (dprobs - delta) * score_scale).astype(jnp.bfloat16)
    grad_q = jnp.einsum(
        "bglm,bmgd->blgd", dscores, k_lines, preferred_element_type=jnp.float32
    ).astype(jnp.bfloat16)
    grad_k = jnp.einsum(
        "bglm,blgd->bmgd", dscores, q_lines, preferred_element_type=jnp.float32
    ).astype(jnp.bfloat16)
    grad_v = jnp.einsum(
        "bglm,blgd->bmgd", probs_low, u_lines, preferred_element_type=jnp.float32
    ).astype(jnp.bfloat16)
    return (output, grad_q, grad_k, grad_v)


def depth_attention(received):
    line_view = received.transpose(1, 0, 2, 3, 4)
    results = line_grads(
        line_view[:, :, 0], line_view[:, :, 1], line_view[:, :, 2], line_view[:, :, 3]
    )
    returned = jnp.stack(results, axis=2).transpose(1, 0, 2, 3, 4)
    return lax.all_to_all(returned, "slab", split_axis=0, concat_axis=1, tiled=True)


def per_device(tokens, cotangent, weights, norm_gain, norm_bias):
    z_planes, rows_x, width_y, feature_count = tokens.shape
    local_w = lax.all_gather(weights, "slab", axis=0, tiled=True)
    full_w = lax.all_gather(local_w, "head", axis=2, tiled=True)
    per_dev = local_w.shape[2]
    head_dim = HD
    groups = per_dev // head_dim
    tok_rows = tokens.astype(jnp.float32)
    tok_mean = jnp.mean(tok_rows, axis=-1, keepdims=True)
    centred = tok_rows - tok_mean
    inv_std = lax.rsqrt(jnp.mean(centred * centred, axis=-1, keepdims=True) + 1e-05)
    normalised = centred * inv_std
    normed = (normalised * norm_gain + norm_bias).astype(jnp.bfloat16)
    plane_h, plane_cot = (
        lax.all_gather(normed, "head", axis=1, tiled=True),
        lax.all_gather(cotangent, "head", axis=1, tiled=True),
    )
    upstream = jnp.einsum(
        "zxyd,dj->zxyj", plane_cot, local_w[:, 3], preferred_element_type=jnp.float32
    ).astype(jnp.bfloat16)
    projected = jnp.einsum(
        "zxyd,dcj->zxycj", plane_h, local_w[:, :3], preferred_element_type=jnp.float32
    ).astype(jnp.bfloat16)
    full_x = plane_h.shape[1]
    head_shape = (z_planes, full_x, width_y, groups, head_dim)
    inputs = [
        projected[:, :, :, 0].reshape(head_shape),
        projected[:, :, :, 1].reshape(head_shape),
        projected[:, :, :, 2].reshape(head_shape),
        upstream.reshape(head_shape),
    ]

    def along_x(tensor):
        return tensor.transpose(0, 2, 1, 3, 4).reshape(z_planes * width_y, full_x, groups, head_dim)

    def from_x(tensor):
        return tensor.reshape(z_planes, width_y, full_x, groups, head_dim).transpose(0, 2, 1, 3, 4)

    x_results = [from_x(tensor) for tensor in line_grads(*[along_x(tensor) for tensor in inputs])]
    y_view = [tensor.reshape(z_planes * full_x, width_y, groups, head_dim) for tensor in inputs]
    y_results = [tensor.reshape(head_shape) for tensor in line_grads(*y_view)]
    plane_cells = full_x * width_y
    packed = jnp.stack(inputs, axis=3).reshape(z_planes, plane_cells, 4, groups, head_dim)
    z_packed = depth_attention(
        lax.all_to_all(packed, "slab", split_axis=1, concat_axis=0, tiled=True)
    )
    z_results = [z_packed[:, :, slot_id].reshape(head_shape) for slot_id in range(4)]
    summed = [
        (
            x_results[slot_id].astype(jnp.float32)
            + y_results[slot_id].astype(jnp.float32)
            + z_results[slot_id].astype(jnp.float32)
        )
        .astype(jnp.bfloat16)
        .reshape(z_planes, full_x, width_y, per_dev)
        for slot_id in range(4)
    ]
    attended = summed[0]
    grads_qkv = jnp.stack(summed[1:], axis=3)
    grad_rows = lax.all_to_all(grads_qkv, "head", split_axis=1, concat_axis=4, tiled=True)
    qkv_part = jnp.einsum("zxyd,zxycj->dcj", plane_h, grads_qkv, preferred_element_type=jnp.float32)
    out_part = jnp.einsum("zxyd,zxyj->dj", plane_cot, attended, preferred_element_type=jnp.float32)
    grad_weights = lax.psum_scatter(
        jnp.concatenate([qkv_part, out_part[:, None, :]], axis=1),
        "slab",
        scatter_dimension=0,
        tiled=True,
    )
    grad_normed = jnp.einsum(
        "zxycj,dcj->zxyd", grad_rows, full_w[:, :3], preferred_element_type=jnp.float32
    )
    gain_part = jnp.sum(grad_normed * normalised, axis=(0, 1, 2))
    bias_part = jnp.sum(grad_normed, axis=(0, 1, 2))
    gain_sum, bias_sum = lax.psum((gain_part, bias_part), ("slab", "head"))
    grad_norm = jnp.stack([gain_sum, bias_sum])
    scaled = grad_normed * norm_gain
    mean_g = jnp.mean(scaled, axis=-1, keepdims=True)
    mean_gx = jnp.mean(scaled * normalised, axis=-1, keepdims=True)
    grad_tokens = (
        cotangent.astype(jnp.float32) + inv_std * (scaled - mean_g - normalised * mean_gx)
    ).astype(jnp.bfloat16)
    return (grad_tokens, grad_weights, grad_norm)


def solution(mesh):
    return jax.shard_map(
        per_device,
        mesh=mesh,
        in_specs=(
            P("slab", "head", None, None),
            P("slab", "head", None, None),
            P("slab", None, "head"),
            P(),
            P(),
        ),
        out_specs=(P("slab", "head", None, None), P("slab", None, "head"), P()),
        check_vma=False,
    )
```

profile of v0, /device:TPU:1, one launch (start us, length us, event | category | flops | bytes accessed | tf_op | source)
XLA Modules:
  0.0 1370.5 jit_solution(2405417070546054507)
XLA Ops:
  9.0 1.1 fusion.103
  10.1 1.8 fusion.123
  11.9 151.1 %all_gather.13 = bf16[768,4,64]{2,1,0:T(4,128)(2,1)S(1)} all-gather(bf16[12,4,64]{2,1,0:T(4,128)(2,1)} %param.7), channel_id=1, replica_groups=mesh['slab'=64,'head'=8] {'slab'}, dimensions={0}, use_global_device_ids=true | all-gather | bytes 399360 | tf_op jit(solution)/shard_map/all_gather | solution.py:46
  164.3 2.0 convolution_convert_fusion.8
  166.7 55.2 %all-gather.4.cloned.1.call-done = bf16[1,64,16,768]{3,2,0,1:T(8,128)(2,1)} async-done(((bf16[1,8,16,768]{3,2,0,1:T(8,128)(2,1)}), bf16[1,64,16,768]{3,2,0,1:T(8,128)(2,1)}) %all-gather.4.cloned.1.call-update) | async-done | bytes 1572880 | tf_op jit(solution)/shard_map/all_gather | solution.py:58
  221.9 2.4 fusion.17
  226.5 3.0 fusion.195
  229.5 1.5 reshape.493
  231.0 7.8 all-to-all-start
  239.0 1.2 copy.170
  240.3 41.4 %all-to-all-done = bf16[64,2,2048]{2,1,0:T(2,128)(2,1)S(1)} async-done(((bf16[64,2,2048]{2,1,0:T(2,128)(2,1)}), bf16[64,2,2048]{2,1,0:T(2,128)(2,1)S(1)}, u32[]{:S(2)}, u32[]{:S(2)}) %all-to-all-start) | async-done | bytes 524320 | tf_op jit(solution)/shard_map/all_to_all | solution.py:88
  286.6 1.6 copy.157
  288.2 1.6 reshape.495
  289.8 7.8 all-to-all-start.1
  305.0 1.1 fusion.196
  306.2 1.2 fusion.194
  307.3 87.0 %all-to-all-done.1 = bf16[64,2,2048]{2,1,0:T(2,128)(2,1)S(1)} async-done(((bf16[64,2,2048]{2,1,0:T(2,128)(2,1)}), bf16[64,2,2048]{2,1,0:T(2,128)(2,1)S(1)}, u32[]{:S(2)}, u32[]{:S(2)}) %all-to-all-start.1) | async-done | bytes 524320 | tf_op jit(solution)/shard_map/all_to_all | solution.py:41
  396.1 2.0 fusion.46
  398.1 2.7 fusion.56
  400.8 1.2 fusion.62
  402.0 1.1 fusion.170
  404.4 1.3 reshape.497
  405.7 6.4 all-to-all-start.2
  412.4 3.0 fusion.23
  416.5 2.1 fusion.70
  418.6 1.6 copy.179
  420.3 1.3 dynamic-slice
  422.2 5.6 copy.201
  427.8 824.3 %all-reduce.4.cloned.1.call-done = f32[768,4,64]{2,1,0:T(4,128)} async-done(((f32[768,4,64]{2,1,0:T(4,128)}), f32[768,4,64]{2,1,0:T(4,128)}) %all-reduce.4.cloned.1.call-update) | async-done | bytes 786448
  1252.1 1.3 constant_dynamic-slice_fusion
  1255.0 2.7 fusion.102
  1257.9 104.6 %all-reduce.1 = (f32[1,768]{1,0:T(1,128)S(1)}, f32[1,768]{1,0:T(1,128)S(1)}) all-reduce(f32[1,768]{1,0:T(1,128)S(1)} %stack.50, f32[1,768]{1,0:T(1,128)S(1)} %stack.49), channel_id=1, replica_groups=mesh['slab'=64,'head'=8] {'slab','head'}, use_global_device_ids=true, to_apply=%region_17.0 | all-reduce | flops 1536 | bytes 12288 | tf_op jit(solution)/shard_map/psum | solution.py:117
  (88 shorter events, 25.6 us)
Async XLA Ops:
  7.2 157.1 %all-gather.6.cloned.1.call-start = ((), (), s32[]{:S(2)}) async-start(), calls=%async_computation.4 | async-start | bytes 1769472 | tf_op jit(solution)/shard_map/all_gather | solution.py:59
  7.9 214.0 %all-gather.4.cloned.1.call-start = ((), (), s32[]{:S(2)}) async-start(), calls=%async_computation.3 | async-start | bytes 1769472 | tf_op jit(solution)/shard_map/all_gather | solution.py:58
  231.0 50.7 %all-to-all-start = ((bf16[64,2,2048]{2,1,0:T(2,128)(2,1)}), bf16[64,2,2048]{2,1,0:T(2,128)(2,1)S(1)}, u32[]{:S(2)}, u32[]{:S(2)}) async-start(bf16[64,2,2048]{2,1,0:T(2,128)(2,1)} %reshape.493), calls=%async_computation | async-start | bytes 1048576 | tf_op jit(solution)/shard_map/all_to_all | solution.py:88
  238.8 183.4 %all-gather.8.cloned.1.call-start = ((), (), s32[]{:S(2)}) async-start(), calls=%async_computation.5 | async-start | bytes 3538944 | tf_op jit(solution)/shard_map/all_gather | solution.py:47
  285.3 1.0 copy-start.10
  289.8 104.5 %all-to-all-start.1 = ((bf16[64,2,2048]{2,1,0:T(2,128)(2,1)}), bf16[64,2,2048]{2,1,0:T(2,128)(2,1)S(1)}, u32[]{:S(2)}, u32[]{:S(2)}) async-start(bf16[64,2,2048]{2,1,0:T(2,128)(2,1)} %reshape.495), calls=%async_computation.1 | async-start | bytes 1048576 | tf_op jit(solution)/shard_map/all_to_all | solution.py:41
  302.6 1.5 copy-start.4
  302.6 1.8 copy-start.3
  303.2 1.6 copy-start.2
  398.1 2.7 copy-start.9
  400.8 1.2 copy-start.7
  405.7 847.8 %all-to-all-start.2 = ((bf16[8,2,12288]{2,1,0:T(2,128)(2,1)}), bf16[8,2,12288]{2,1,0:T(2,128)(2,1)S(1)}, u32[]{:S(2)}, u32[]{:S(2)}) async-start(bf16[8,2,12288]{2,1,0:T(2,128)(2,1)} %reshape.497), calls=%async_computation.2 | async-start | bytes 786432 | tf_op jit(solution)/shard_map/all_to_all | solution.py:103
  412.1 4.4 copy-start.1
  412.1 4.4 copy-start.8
  412.1 840.0 %all-reduce.4.cloned.1.call-start = ((), (), s32[]{:S(2)}) async-start(), calls=%async_computation.6 | async-start | bytes 3145728
  416.5 2.1 copy-start.6
  1254.0 1.0 copy-start
  1254.0 1.0 copy-start.11
  1255.0 108.0 %copy-start.5 = (bf16[1,8,16,768]{3,2,1,0:T(8,128)(2,1)S(1)}, bf16[1,8,16,768]{3,2,1,0:T(8,128)(2,1)}, u32[]{:S(2)}) copy-start(bf16[1,8,16,768]{3,2,1,0:T(8,128)(2,1)} %param.6) | copy-start | bytes 589828
Sparse Core Ops, SparseCore 0:
  11.2 110.2 all-gather.5
  125.3 96.5 all-gather.3
  242.8 112.5 all-gather.7
  420.4 831.7 all-reduce.3
where the time goes:
time: 1370 us
  waiting for transfers between devices  1010 us (74%)
  blocking collectives  256 us (19%)
  local copies, waits for them, and re-layouts  33.6 us (2%)
  matrix products  25.1 us (2%)
  starting transfers between devices  22.5 us (2%)
  between operations  14.9 us (1%)
    unnamed x5, waiting for transfers between devices  825 us
    all_gather x1, blocking collectives, per_device(): local_w = lax.all_gather(weights, 'slab', axis=0, tiled=True)  151 us
    psum x1, blocking collectives, per_device(): gain_sum, bias_sum = lax.psum((gain_part, bias_part), ('slab', 'head'))  105 us
    all_to_all x1, waiting for transfers between devices, depth_attention(): lax.all_to_all(returned, 'slab', split_axis=0, concat_axis=1, tiled=True)  87 us
    all_gather x1, waiting for transfers between devices, per_device(): lax.all_gather(normed, 'head', axis=1, tiled=True)  55.2 us
    all_to_all x1, waiting for transfers between devices, per_device(): lax.all_to_all(packed, 'slab', split_axis=1, concat_axis=0, tiled=True)  41.4 us
  transfers between devices with their start and end apart: 7, of which 4 were waited for; matrix products, arithmetic and copies ran while one was open for 4% of the time, Pallas kernels for 0%

commit v1 on v0

v1 whole, which is shorter than its diff:
```python
import jax
import jax.numpy as jnp
from jax import lax
from jax.experimental import pallas as pl
from jax.experimental.pallas import tpu as pltpu
from jax.sharding import PartitionSpec as P

MESH = pl.DeviceIdType.MESH
BF = jnp.bfloat16
F32 = jnp.float32
EPS = 1e-05
SCALE = 0.125


def one_hot(rows, cols, source):
    dest = lax.broadcasted_iota(jnp.int32, (rows, cols), 0)
    src = lax.broadcasted_iota(jnp.int32, (rows, cols), 1)
    return (source(dest) == src).astype(BF)


def dot(a, b):
    return jnp.dot(a, b, preferred_element_type=F32)


def dot_nt(a, b):
    return lax.dot_general(a, b, (((1,), (1,)), ((), ())), preferred_element_type=F32)


def dot_tn(a, b):
    return lax.dot_general(a, b, (((0,), (0,)), ((), ())), preferred_element_type=F32)


def kernel(
    tok, cot, wpiece, gain, bias,
    out_tok, out_w, out_norm,
    wq, wb_piece, zw, wb,
    send_rows, p1, xb, zv, zb,
    lt, gs, nrm_y, inv_y, gn_acc, gn_y,
    gx, xg, gz, zg, rb, ret,
    gw_send, gw_recv, gw_own, ys, yr, yacc, xs, xr, zs, zr,
    nc, ny_, nx_, nz_,
    s_q, r_q, s_wz, r_wz, s_wx, r_wx, s_wy, r_wy, s_wc, r_wc,
    s_p1, r_p1, s_2a, r_2a, s_2b, r_2b,
    s_gx, r_gx, s_gz, r_gz, s_rt, r_rt,
    s_c, r_c, s_y, r_y, s_x, r_x, s_z, r_z, s_f, r_f,
    s_nc, r_nc, s_ny, r_ny, s_nx, r_nx, s_nz, r_nz,
):
    slab = lax.axis_index("slab")
    head = lax.axis_index("head")
    z_lo, x, core = slab // 8, (slab // 2) % 4, slab % 2
    y, z_hi = head // 2, head % 2
    z = z_hi * 8 + z_lo
    k = x * 2 + core
    xp = x // 2
    member = (x % 2) * 2 + core

    def at_z(c):
        return ((c % 8) * 8 + k, y * 2 + c // 8)

    def at_y(v):
        return (slab, v * 2 + z_hi)

    def at_k(v):
        return (z_lo * 8 + v, head)

    def rcopy(src, dst, ssem, rsem, dev):
        return pltpu.make_async_remote_copy(
            src_ref=src, dst_ref=dst, send_sem=ssem, recv_sem=rsem, device_id=dev, device_id_type=MESH
        )

    def arrived(dst, rsem, ssem, dev):
        rcopy(dst, dst, ssem, rsem, dev).wait_recv()

    barrier = pltpu.get_barrier_semaphore()

    @pl.loop(1, 16)
    def _(d):
        pl.semaphore_signal(barrier, inc=1, device_id=at_z((z + d) % 16), device_id_type=MESH)

    for d in range(1, 4):
        pl.semaphore_signal(barrier, inc=1, device_id=at_y((y + d) % 4), device_id_type=MESH)
    for d in range(1, 8):
        pl.semaphore_signal(barrier, inc=1, device_id=at_k((k + d) % 8), device_id_type=MESH)
    pl.semaphore_wait(barrier, 25)

    wq[member] = wpiece[...]
    sends = []

    def go(copy):
        copy.start()
        sends.append(copy)

    def quad(d):
        other = (member + d) % 4
        return other, at_k(((x // 2) * 2 + other // 2) * 2 + other % 2)

    for d in range(1, 4):
        other, dev = quad(d)
        go(rcopy(wq.at[member], wq.at[member], s_q.at[d], r_q.at[member], dev))

    perm = one_hot(128, 128, lambda i: (i % 8) * 16 + i // 8)
    t_rows = dot(perm, tok[...])
    c_rows = dot(perm, cot[...])
    send_rows[...] = jnp.concatenate(
        [t_rows.reshape(16, 8, 768), c_rows.reshape(16, 8, 768)], axis=1
    ).astype(BF)

    for d in range(1, 4):
        other, dev = quad(d)
        arrived(wq.at[other], r_q.at[other], s_q.at[d], dev)
    stack = one_hot(48, 64, lambda i: (i // 12) * 16 + i % 12)
    block = dot(stack, wq[...].reshape(64, 256)).astype(BF)
    wb_piece[0] = block[:, :128]
    wb_piece[1] = block[:, 128:]
    zw[z_lo, z_hi] = wb_piece[core]

    @pl.loop(1, 16)
    def _(d):
        c = (z + d) % 16
        rcopy(wb_piece.at[core], zw.at[z_lo, z_hi], s_wz.at[d], r_wz.at[z], at_z(c)).start()

    p1[z_lo, z_hi] = send_rows[z]

    @pl.loop(1, 16)
    def _(d):
        c = (z + d) % 16
        rcopy(send_rows.at[c], p1.at[z_lo, z_hi], s_p1.at[d], r_p1.at[z], at_z(c)).start()

    @pl.loop(1, 16)
    def _(d):
        c = (z + d) % 16
        arrived(zw.at[c % 8, c // 8], r_wz.at[c], s_wz.at[d], at_z(c))

    for c2 in range(2):
        merged = sum(
            dot(
                zw[:, zh].reshape(384, 128),
                lane_map(c2, zh),
            )
            for zh in range(2)
        )
        wb[core, y, c2, :, xp] = merged.astype(BF).reshape(8, 48, 128)
    mate = (3 - x) * 2 + core
    go(rcopy(wb.at[core, y, :, :, xp], wb.at[core, y, :, :, xp], s_wx, r_wx, at_k(mate)))
    arrived(wb.at[core, y, :, :, 1 - xp], r_wx, s_wx, at_k(mate))
    for d in range(1, 4):
        go(rcopy(wb.at[core, y], wb.at[core, y], s_wy.at[d], r_wy.at[y], at_y((y + d) % 4)))
    pair = at_k(x * 2 + 1 - core)
    go(rcopy(wb.at[core, y], wb.at[core, y], s_wc.at[0], r_wc.at[y], pair))

    @pl.loop(1, 16)
    def _(d):
        c = (z + d) % 16
        arrived(p1.at[c % 8, c // 8], r_p1.at[c], s_p1.at[d], at_z(c))

    for d in range(1, 4):
        v = (y + d) % 4
        go(rcopy(p1.at[pl.ds(2 * v, 2)], xb.at[:, y], s_2a.at[d], r_2a.at[y], at_y(v)))
    xb[:, y] = p1[pl.ds(2 * y, 2)]
    perm_v = one_hot(
        256, 256, lambda i: (i % 8) * 32 + (i // 128) * 16 + ((i // 8) % 2) * 8 + (i // 16) % 8
    )
    zv[...] = dot(perm_v, p1[...].reshape(256, 768)).astype(BF).reshape(8, 2, 16, 768)
    for d in range(1, 8):
        v = (k + d) % 8
        go(rcopy(zv.at[v], zb.at[:, k], s_2b.at[d], r_2b.at[k], at_k(v)))
    zb[:, k] = zv[k]

    for d in (1, 3, 2):
        v = (y + d) % 4
        arrived(wb.at[core, v], r_wy.at[v], s_wy.at[d], at_y(v))
        go(rcopy(wb.at[core, v], wb.at[core, v], s_wc.at[d], r_wc.at[v], pair))
    for d in range(4):
        v = (y + d) % 4
        arrived(wb.at[1 - core, v], r_wc.at[v], s_wc.at[d], pair)

    gain_row, bias_row = gain[...], bias[...]
    row_i = lax.broadcasted_iota(jnp.int32, (128, 128), 0)
    col_i = lax.broadcasted_iota(jnp.int32, (128, 128), 1)

    def home(idx, rows, same):
        f = rows.astype(F32)
        t = f[:, :8].reshape(128, 768)
        c16 = f[:, 8:].reshape(128, 768).astype(BF)
        centred = t - jnp.mean(t, axis=-1, keepdims=True)
        inv = lax.rsqrt(jnp.mean(centred * centred, axis=-1, keepdims=True) + EPS)
        nrm = centred * inv
        normed = (nrm * gain_row + bias_row).astype(BF)
        lt[0, :, idx * 128:(idx + 1) * 128] = normed.T
        lt[1, :, idx * 128:(idx + 1) * 128] = c16.T
        gn_acc[...] = jnp.zeros_like(gn_acc)

        @pl.loop(0, 2)
        def _(hq):
            def w_of(c):
                parts = [wb[c // 2, 2 * hq + e, c % 2].reshape(768, 128) for e in range(2)]
                return jnp.concatenate(parts, axis=1)

            q = dot(normed, w_of(0)).astype(BF)
            kk = dot(normed, w_of(1)).astype(BF)
            v = dot(normed, w_of(2)).astype(BF)
            u = dot(c16, w_of(3)).astype(BF)
            lane_head = lax.broadcasted_iota(jnp.int32, (128, 256), 1) // 64

            def spread(a):
                return jnp.concatenate(
                    [jnp.where(lane_head == j, a, jnp.zeros_like(a)) for j in range(4)], axis=0
                )

            qs, ks, vs, us = spread(q), spread(kk), spread(v), spread(u)
            s = dot_nt(q, ks)
            dp = dot_nt(u, vs)
            lows, dss = [], []
            for j in range(4):
                sj = jnp.where(same, s[:, j * 128:(j + 1) * 128] * SCALE, -1e30)
                e = jnp.exp(sj - jnp.max(sj, axis=-1, keepdims=True))
                pr = e / jnp.sum(e, axis=-1, keepdims=True)
                dpj = dp[:, j * 128:(j + 1) * 128]
                delta = jnp.sum(pr * dpj, axis=-1, keepdims=True)
                dss.append((pr * (dpj - delta) * SCALE).astype(BF))
                lows.append(pr.astype(BF))
            p_wide, ds_wide = jnp.concatenate(lows, axis=1), jnp.concatenate(dss, axis=1)
            p_tall, ds_tall = jnp.concatenate(lows, axis=0), jnp.concatenate(dss, axis=0)
            att = dot(p_wide, vs).astype(BF)
            gq = dot(ds_wide, ks).astype(BF)
            gk = dot_tn(ds_tall, qs).astype(BF)
            gv = dot_tn(p_tall, us).astype(BF)
            for c, g in enumerate((gq, gk, gv, att)):
                gs[c, hq, idx * 128:(idx + 1) * 128, :] = g
            gn_acc[...] += dot_nt(gq, w_of(0)) + dot_nt(gk, w_of(1)) + dot_nt(gv, w_of(2))

        g = gn_acc[...]
        part = jnp.concatenate(
            [jnp.sum(g * nrm, axis=0, keepdims=True), jnp.sum(g, axis=0, keepdims=True)], axis=0
        )
        return g, nrm, inv, part

    g, nrm, inv, norm_part = home(0, send_rows[...], row_i % 8 == col_i % 8)
    gn_y[...] = g
    nrm_y[...] = nrm
    inv_y[...] = jnp.broadcast_to(inv, (128, 128))

    for d in range(1, 4):
        v = (y + d) % 4
        arrived(xb.at[:, v], r_2a.at[v], s_2a.at[d], at_y(v))
    half = row_i // 64 == col_i // 64
    g, _, _, part = home(1, xb[...].reshape(16, 16, 768), half)
    norm_part = norm_part + part
    gx[...] = g.astype(BF).reshape(2, 4, 16, 768)
    for d in range(1, 4):
        v = (y + d) % 4
        go(rcopy(gx.at[:, v], xg.at[pl.ds(2 * y, 2)], s_gx.at[d], r_gx.at[y], at_y(v)))
    xg[pl.ds(2 * y, 2)] = gx[:, y]

    for d in range(1, 8):
        v = (k + d) % 8
        arrived(zb.at[:, v], r_2b.at[v], s_2b.at[d], at_k(v))
    g, _, _, part = home(2, zb[...].reshape(16, 16, 768), half)
    norm_part = norm_part + part
    g4 = g.reshape(2, 8, 8, 768)
    gz[...] = jnp.concatenate([g4[0], g4[1]], axis=1).astype(BF)
    for d in range(1, 8):
        v = (k + d) % 8
        go(rcopy(gz.at[v], zg.at[k], s_gz.at[d], r_gz.at[k], at_k(v)))
    zg[k] = gz[k]

    nc[core] = norm_part
    go(rcopy(nc.at[core], nc.at[core], s_nc, r_nc, pair))

    def weight_grad(c, hq):
        return dot(lt[jnp.where(c == 3, 1, 0)], gs[c, hq])

    for hq in range(2):
        for c2 in range(2):
            full = weight_grad(2 * (1 - core) + c2, hq).astype(BF)
            gw_send[2 * hq, c2] = full[:, :128]
            gw_send[2 * hq + 1, c2] = full[:, 128:]
        for e in range(2):
            v = 2 * hq + e
            go(rcopy(gw_send.at[v], gw_recv.at[v], s_c.at[v], r_c.at[v], pair))
    for hq in range(2):
        for c2 in range(2):
            full = weight_grad(2 * core + c2, hq)
            gw_own[2 * hq, c2] = full[:, :128]
            gw_own[2 * hq + 1, c2] = full[:, 128:]

    for d in range(1, 4):
        v = (y + d) % 4
        arrived(xg.at[pl.ds(2 * v, 2)], r_gx.at[v], s_gx.at[d], at_y(v))
    for d in range(1, 8):
        v = (k + d) % 8
        arrived(zg.at[v], r_gz.at[v], s_gz.at[d], at_k(v))
    perm_g = one_hot(128, 128, lambda i: (i % 16) * 8 + i // 16)
    total = dot(perm_g, zg[...].reshape(128, 768)) + xg[...].reshape(128, 768).astype(F32)
    total = total.reshape(16, 8, 768)
    rb[...] = jnp.concatenate([total[:, :, :384], total[:, :, 384:]], axis=1).astype(BF)

    @pl.loop(1, 16)
    def _(d):
        c = (z + d) % 16
        rcopy(rb.at[(c % 8) * 2 + c // 8], ret.at[z], s_rt.at[d], r_rt.at[z], at_z(c)).start()

    ret[z] = rb[z_lo * 2 + z_hi]

    for d in (2, 1, 3, 0):
        v = (y + d) % 4
        arrived(gw_recv.at[v], r_c.at[v], s_c.at[v], pair)
        ys[v] = (gw_own[v] + gw_recv[v].astype(F32)).astype(BF)
        if d:
            go(rcopy(ys.at[v], yr.at[y], s_y.at[d], r_y.at[y], at_y(v)))
    yr[y] = ys[y]
    arrived(nc.at[1 - core], r_nc, s_nc, pair)
    ny_[y] = nc[0] + nc[1]
    for d in range(1, 4):
        go(rcopy(ny_.at[y], ny_.at[y], s_ny.at[d], r_ny.at[y], at_y((y + d) % 4)))
    for d in range(1, 4):
        v = (y + d) % 4
        arrived(yr.at[v], r_y.at[v], s_y.at[d], at_y(v))
        arrived(ny_.at[v], r_ny.at[v], s_ny.at[d], at_y(v))
    y_total = yr[0].astype(F32) + yr[1].astype(F32) + yr[2].astype(F32) + yr[3].astype(F32)
    yacc[...] = y_total.astype(BF).reshape(2, 8, 2, 48, 128)
    nx_[x] = (ny_[0] + ny_[1]) + (ny_[2] + ny_[3])

    for d in (2, 1, 3, 0):
        v = (x + d) % 4
        xs[v] = yacc[v % 2, :, v // 2]
        if d:
            dev = at_k(v * 2 + core)
            go(rcopy(xs.at[v], xr.at[x], s_x.at[d], r_x.at[x], dev))
            go(rcopy(nx_.at[x], nx_.at[x], s_nx.at[d], r_nx.at[x], dev))
    xr[x] = xs[x]
    for d in range(1, 4):
        v = (x + d) % 4
        dev = at_k(v * 2 + core)
        arrived(xr.at[v], r_x.at[v], s_x.at[d], dev)
        arrived(nx_.at[v], r_nx.at[v], s_nx.at[d], dev)
    x_total = xr[0].astype(F32) + xr[1].astype(F32) + xr[2].astype(F32) + xr[3].astype(F32)
    zs[...] = x_total.astype(BF)
    nz_[z] = (nx_[0] + nx_[1]) + (nx_[2] + nx_[3])

    @pl.loop(1, 16)
    def _(d):
        c = (z + d) % 16
        rcopy(zs.at[c % 8], zr.at[z], s_z.at[d], r_z.at[z], at_z(c)).start()
        rcopy(nz_.at[z], nz_.at[z], s_nz.at[d], r_nz.at[z], at_z(c)).start()

    zr[z] = zs[z_lo]

    @pl.loop(1, 16)
    def _(d):
        c = (z + d) % 16
        arrived(ret.at[c], r_rt.at[c], s_rt.at[d], at_z(c))

    back = ret[...].astype(F32)
    back = jnp.concatenate([back[:, :8], back[:, 8:]], axis=2).reshape(128, 768)
    grad_normed = gn_y[...] + back
    scaled = grad_normed * gain_row
    nrm = nrm_y[...]
    m1 = jnp.mean(scaled, axis=-1, keepdims=True)
    m2 = jnp.mean(scaled * nrm, axis=-1, keepdims=True)
    c_rows = send_rows[...].astype(F32)[:, 8:].reshape(128, 768)
    rows = (c_rows + inv_y[:, :1] * (scaled - m1 - nrm * m2)).astype(BF)
    perm_b = one_hot(128, 128, lambda i: (i % 16) * 8 + i // 16)
    out_tok[...] = dot(perm_b, rows).astype(BF)

    @pl.loop(1, 16)
    def _(d):
        c = (z + d) % 16
        arrived(zr.at[c], r_z.at[c], s_z.at[d], at_z(c))
        arrived(nz_.at[c], r_nz.at[c], s_nz.at[d], at_z(c))

    z_total = zr[0].astype(F32)
    norm_total = nz_[0]
    for c in range(1, 16):
        z_total = z_total + zr[c].astype(F32)
        norm_total = norm_total + nz_[c]
    out_norm[...] = norm_total

    mine = 2 * core + x % 2
    out_w[mine] = z_total
    for d in range(1, 4):
        other, dev = quad(d)
        go(rcopy(out_w.at[mine], out_w.at[mine], s_f.at[d], r_f.at[mine], dev))
    for d in range(1, 4):
        other, dev = quad(d)
        theirs = 2 * (other % 2) + other // 2
        arrived(out_w.at[theirs], r_f.at[theirs], s_f.at[d], dev)

    for copy in sends:
        copy.wait_send()

    @pl.loop(1, 16)
    def _(d):
        c = (z + d) % 16
        dev = at_z(c)
        rcopy(wb_piece.at[core], zw.at[z_lo, z_hi], s_wz.at[d], r_wz.at[z], dev).wait_send()
        rcopy(send_rows.at[c], p1.at[z_lo, z_hi], s_p1.at[d], r_p1.at[z], dev).wait_send()
        rcopy(rb.at[(c % 8) * 2 + c // 8], ret.at[z], s_rt.at[d], r_rt.at[z], dev).wait_send()
        rcopy(zs.at[c % 8], zr.at[z], s_z.at[d], r_z.at[z], dev).wait_send()
        rcopy(nz_.at[z], nz_.at[z], s_nz.at[d], r_nz.at[z], dev).wait_send()


def lane_map(c2, zh):
    src = lax.broadcasted_iota(jnp.int32, (128, 128), 0)
    dest = lax.broadcasted_iota(jnp.int32, (128, 128), 1)
    return ((dest // 64 == zh) & (src == c2 * 64 + dest % 64)).astype(BF)


def per_device(tokens, cotangent, weights, norm_gain, norm_bias):
    tok = tokens.reshape(128, 768)
    cot = cotangent.reshape(128, 768)
    piece = jnp.pad(weights.reshape(12, 256), ((0, 4), (0, 0)))
    vm = pltpu.VMEM
    dma = pltpu.SemaphoreType.DMA
    scratch = [
        vm((4, 16, 256), BF),
        vm((2, 48, 128), BF),
        vm((8, 2, 48, 128), BF),
        vm((2, 4, 2, 8, 2, 48, 128), BF),
        vm((16, 16, 768), BF),
        vm((8, 2, 16, 768), BF),
        vm((2, 4, 2, 16, 768), BF),
        vm((8, 2, 16, 768), BF),
        vm((2, 8, 16, 768), BF),
        vm((2, 768, 384), BF),
        vm((4, 2, 384, 256), BF),
        vm((128, 768), F32),
        vm((128, 128), F32),
        vm((128, 768), F32),
        vm((128, 768), F32),
        vm((2, 4, 16, 768), BF),
        vm((8, 16, 768), BF),
        vm((8, 16, 768), BF),
        vm((8, 16, 768), BF),
        vm((16, 16, 384), BF),
        vm((16, 16, 384), BF),
        vm((4, 2, 768, 128), BF),
        vm((4, 2, 768, 128), BF),
        vm((4, 2, 768, 128), F32),
        vm((4, 2, 768, 128), BF),
        vm((4, 2, 768, 128), BF),
        vm((2, 8, 2, 48, 128), BF),
        vm((4, 8, 48, 128), BF),
        vm((4, 8, 48, 128), BF),
        vm((8, 48, 128), BF),
        vm((16, 48, 128), BF),
        vm((2, 2, 768), F32),
        vm((4, 2, 768), F32),
        vm((4, 2, 768), F32),
        vm((16, 2, 768), F32),
        dma((4,)), dma((4,)),
        dma((16,)), dma((16,)),
        dma, dma,
        dma((4,)), dma((4,)),
        dma((4,)), dma((4,)),
        dma((16,)), dma((16,)),
        dma((4,)), dma((4,)),
        dma((8,)), dma((8,)),
        dma((4,)), dma((4,)),
        dma((8,)), dma((8,)),
        dma((16,)), dma((16,)),
        dma((4,)), dma((4,)),
        dma((4,)), dma((4,)),
        dma((4,)), dma((4,)),
        dma((16,)), dma((16,)),
        dma((4,)), dma((4,)),
        dma, dma,
        dma((4,)), dma((4,)),
        dma((4,)), dma((4,)),
        dma((16,)), dma((16,)),
    ]
    whole = pl.BlockSpec(memory_space=pltpu.VMEM)
    grad_tok, grad_w, grad_norm = pl.pallas_call(
        kernel,
        out_shape=(
            jax.ShapeDtypeStruct((128, 768), BF),
            jax.ShapeDtypeStruct((4, 48, 128), F32),
            jax.ShapeDtypeStruct((2, 768), F32),
        ),
        in_specs=[whole] * 5,
        out_specs=(whole, whole, whole),
        scratch_shapes=scratch,
        compiler_params=pltpu.CompilerParams(
            collective_id=0, has_side_effects=True, vmem_limit_bytes=52 * 1024 * 1024
        ),
        name="axial_backward",
    )(tok, cot, piece, norm_gain.reshape(1, 768), norm_bias.reshape(1, 768))
    slab = lax.axis_index("slab")
    head = lax.axis_index("head")
    mine = lax.dynamic_slice(grad_w, (0, (slab % 4) * 12, (head % 2) * 64), (4, 12, 64))
    return grad_tok.reshape(tokens.shape), mine.transpose(1, 0, 2), grad_norm


def solution(mesh):
    return jax.shard_map(
        per_device,
        mesh=mesh,
        in_specs=(
            P("slab", "head", None, None),
            P("slab", "head", None, None),
            P("slab", None, "head"),
            P(),
            P(),
        ),
        out_specs=(P("slab", "head", None, None), P("slab", None, "head"), P()),
        check_vma=False,
    )
```

time: 1370 us -> 129 us (0.09)
  waiting for transfers between devices: 1010 us -> 0 us
  blocking collectives: 256 us -> 0 us
  Pallas kernels: 0 us -> 122 us
  local copies, waits for them, and re-layouts: 33.6 us -> 5.98 us
  matrix products: 25.1 us -> 0 us
  starting transfers between devices: 22.5 us -> 0 us
  between operations: 14.9 us -> 0.69 us
    unnamed x5 -> x0, waiting for transfers between devices: 825 us -> none
    all_gather x1 -> x0, blocking collectives: 151 us -> none  [per_device(): local_w = lax.all_gather(weights, 'slab', axis=0, tiled=True)]
    all_to_all x3 -> x0, waiting for transfers between devices: 128 us -> none  [the longest x1 87 us: depth_attention(): lax.all_to_all(returned, 'slab', split_axis=0, concat_axis=1, tiled=True)]
    pallas_call x0 -> x1, Pallas kernels: none -> 122 us  [per_device(): pl.pallas_call(kernel, out_shape=(jax.ShapeDtypeStruct((128, 768), BF), j...]
    psum x1 -> x0, blocking collectives: 105 us -> none  [per_device(): gain_sum, bias_sum = lax.psum((gain_part, bias_part), ('slab', 'head'))]
    all_gather x3 -> x0, waiting for transfers between devices: 55.3 us -> none  [the longest x1 55.2 us: per_device(): lax.all_gather(normed, 'head', axis=1, tiled=True)]
    dot_general x19 -> x0, matrix products: 23.2 us -> none  [the longest x3 4.06 us: line_grads(): jnp.einsum('bglm,blgd->bmgd', dscores, q_lines, preferred_element_type=jn...]
    all_to_all x3 -> x0, starting transfers between devices: 21.9 us -> none  [the longest x1 7.78 us: per_device(): lax.all_to_all(packed, 'slab', split_axis=1, concat_axis=0, tiled=True)]
  transfers between devices with their start and end apart: 7 -> 0, of which waited for: 4 -> 0; matrix products, arithmetic and copies ran while one was open for 4% -> 0% of each run, Pallas kernels for 0% -> 0%
where the time goes in v1:
time: 129 us
  Pallas kernels  122 us (95%)
  local copies, waits for them, and re-layouts  5.98 us (5%)
    pallas_call x1, Pallas kernels, per_device(): pl.pallas_call(kernel, out_shape=(jax.ShapeDtypeStruct((128, 768), BF), j...  122 us
    unnamed x13, local copies, waits for them, and re-layouts  5.79 us

profile of v1, /device:TPU:1, one launch (start us, length us, event | category | flops | bytes accessed | tf_op | source)
XLA Modules:
  0.0 128.8 jit_solution(10108099727917378422)
XLA Ops:
  0.6 0.0 copy-start.2
  0.7 0.7 copy-done.2
  1.4 0.1 reshape.26
  1.4 0.0 copy-start.3
  1.5 0.7 copy-done.3
  2.1 0.0 copy-start.4
  2.1 0.7 copy-done.4
  2.8 0.0 copy-start
  2.8 0.9 copy-done
  3.8 0.0 copy-start.1
  3.8 0.9 copy-done.1
  4.7 122.1 %axial_backward.1 = (bf16[128,768]{1,0:T(8,128)(2,1)S(1)}, f32[4,48,128]{2,1,0:T(8,128)S(1)}, f32[2,768]{1,0:T(2,128)S(1)}) custom-call(bf16[128,768]{1,0:T(8,128)(2,1)S(1)} %bitcast.5, bf16[128,768]{1,0:T(8,128)(2,1)S(1)} %bitcast.6, bf16[16,256]{1,0:T(8,128)(2,1)S(1)} %pad.4.wpiece, f32[1,768]{1,0:T(1,128)S(1)} %reshape.27.gain, f32[1,768]{1,0:T(1,128)S(1)} %reshape.28.bias), custom_call_target="tpu_custom_call" | custom-call | tf_op jit(solution)/shard_map/axial_backward/pallas_call | solution.py:473
  126.8 0.1 dynamic-slice_bitcast_fusion
  126.9 0.6 copy.8
  127.5 0.7 copy.11
  128.2 0.6 copy.12
  (3 shorter events, 0.0 us)
Async XLA Ops:
  0.6 0.7 copy-start.2
  1.4 0.7 copy-start.3
  2.1 0.7 copy-start.4
  2.8 0.9 copy-start
  3.8 0.9 copy-start.1

commit v2 on v0

v2 whole, which is shorter than its diff:
```python
import types

import jax
import jax.numpy as jnp
from jax import lax
from jax.experimental import pallas as pl
from jax.experimental.pallas import tpu as pltpu
from jax.sharding import PartitionSpec as P

MESH = pl.DeviceIdType.MESH
BF = jnp.bfloat16
F32 = jnp.float32
EPS = 1e-05
SCALE = 0.125
VM = pltpu.VMEM

BUFFERS = {
    "tok": VM((128, 768), BF),
    "cot": VM((128, 768), BF),
    "wraw": VM((12, 4, 64), BF),
    "gain": VM((768,), F32),
    "bias": VM((768,), F32),
    "wq": VM((4, 16, 256), BF),
    "wpart": VM((2, 48, 128), BF),
    "wb": VM((2, 2, 4, 4, 4, 48, 128), BF),
    "send_rows": VM((16, 16, 768), BF),
    "p1": VM((8, 2, 16, 768), BF),
    "xb": VM((2, 4, 2, 16, 768), BF),
    "zv": VM((8, 2, 16, 768), BF),
    "zb": VM((2, 8, 16, 768), BF),
    "lt": VM((2, 768, 384), BF),
    "gs_qk": VM((2, 384, 512), BF),
    "gs_v": VM((2, 384, 256), BF),
    "gs_a": VM((2, 384, 256), BF),
    "nrm_y": VM((128, 768), F32),
    "inv_y": VM((128, 128), F32),
    "gn_acc": VM((128, 768), F32),
    "gn_y": VM((128, 768), F32),
    "gx": VM((2, 4, 16, 768), BF),
    "xg": VM((8, 16, 768), BF),
    "gz": VM((8, 16, 768), BF),
    "zg": VM((8, 16, 768), BF),
    "rb": VM((8, 2, 16, 384), BF),
    "ret": VM((16, 16, 384), BF),
    "gw_send": VM((2, 4, 768, 128), BF),
    "gw_recv": VM((2, 4, 768, 128), BF),
    "gw_own": VM((2, 4, 768, 128), F32),
    "a1s": VM((4, 768, 128), BF),
    "a1r": VM((4, 768, 128), BF),
    "b1s": VM((4, 4, 4, 48, 128), BF),
    "b1r": VM((4, 4, 4, 48, 128), BF),
    "a2s": VM((4, 4, 48, 128), BF),
    "a2r": VM((4, 4, 48, 128), BF),
    "b2s": VM((4, 4, 48, 128), BF),
    "b2r": VM((4, 4, 48, 128), BF),
    "zs": VM((2, 4, 48, 128), BF),
    "zr": VM((16, 48, 128), BF),
    "qr": VM((2, 48, 128), F32),
    "tok_out": VM((128, 768), BF),
    "norm_out": VM((2, 768), F32),
    "nc": VM((2, 2, 768), F32),
    "ny": VM((4, 2, 768), F32),
    "nx": VM((4, 2, 768), F32),
    "nz": VM((16, 2, 768), F32),
}
SEMAPHORES = {
    "q": 4, "wz": 16, "wa1": 4, "wb1": 4, "wa2": 4, "wb2": 4, "wca": 4, "wcb": 4,
    "p1": 16, "xl": 4, "zl": 8, "gx": 4, "gz": 8, "rt": 16,
    "c": 2, "a1": 4, "b1": 4, "a2": 4, "b2": 4, "z": 16, "f": 4,
    "nc": 2, "ny": 4, "nx": 4, "nz": 16,
}


def one_hot(rows, cols, source):
    dest = lax.broadcasted_iota(jnp.int32, (rows, cols), 0)
    src = lax.broadcasted_iota(jnp.int32, (rows, cols), 1)
    return (source(dest) == src).astype(BF)


def dot(a, b):
    return jnp.dot(a, b, preferred_element_type=F32)


def dot_nt(a, b):
    return lax.dot_general(a, b, (((1,), (1,)), ((), ())), preferred_element_type=F32)


def dot_tn(a, b):
    return lax.dot_general(a, b, (((0,), (0,)), ((), ())), preferred_element_type=F32)


def swap(a, b):
    low = lax.broadcasted_iota(jnp.int32, a.shape, 1) < 64
    return jnp.where(low, a, pltpu.roll(b, 64, 1)), jnp.where(low, pltpu.roll(a, 64, 1), b)


def kernel(tok_in, cot_in, w_in, gain_in, bias_in, tok_res, w_res, norm_res, *refs):
    names = list(BUFFERS)
    r = types.SimpleNamespace(**dict(zip(names, refs)))
    rest = refs[len(names):]
    ssem = {n: rest[2 * i] for i, n in enumerate(SEMAPHORES)}
    rsem = {n: rest[2 * i + 1] for i, n in enumerate(SEMAPHORES)}
    lsem = rest[-1]

    slab = lax.axis_index("slab")
    head = lax.axis_index("head")
    z_lo, x, core = slab // 8, (slab // 2) % 4, slab % 2
    y, z_hi = head // 2, head % 2
    z = z_hi * 8 + z_lo
    k = x * 2 + core
    p = x % 2
    j = 2 * p + x // 2
    member = p * 2 + core
    holder = z_lo % 2 == p

    def at_z(c):
        return ((c % 8) * 8 + k, y * 2 + c // 8)

    def at_y(v):
        return (slab, v * 2 + z_hi)

    def at_k(v):
        return (z_lo * 8 + v, head)

    def at_x(v):
        return at_k(v * 2 + core)

    def j_of(v):
        return 2 * (v % 2) + v // 2

    pair = at_k(x * 2 + 1 - core)

    def rcopy(name, src, dst, si, ri, dev):
        return pltpu.make_async_remote_copy(
            src_ref=src, dst_ref=dst, send_sem=ssem[name].at[si], recv_sem=rsem[name].at[ri],
            device_id=dev, device_id_type=MESH,
        )

    sends = []

    def go(*args):
        copy = rcopy(*args)
        copy.start()
        sends.append(copy)

    def arrived(name, dst, ri, dev):
        rcopy(name, dst, dst, 0, ri, dev).wait_recv()

    loads = [
        pltpu.make_async_copy(src, dst, lsem.at[i])
        for i, (src, dst) in enumerate(
            ((w_in, r.wraw), (tok_in, r.tok), (cot_in, r.cot), (gain_in, r.gain), (bias_in, r.bias))
        )
    ]
    for load in loads:
        load.start()

    barrier = pltpu.get_barrier_semaphore()

    @pl.loop(1, 16)
    def _(d):
        pl.semaphore_signal(barrier, inc=1, device_id=at_z((z + d) % 16), device_id_type=MESH)

    for d in range(1, 4):
        pl.semaphore_signal(barrier, inc=1, device_id=at_y((y + d) % 4), device_id_type=MESH)
    for d in range(1, 8):
        pl.semaphore_signal(barrier, inc=1, device_id=at_k((k + d) % 8), device_id_type=MESH)

    loads[0].wait()
    wide = jnp.concatenate([r.wraw[:, c, :].astype(F32) for c in range(4)], axis=1)
    wide = jnp.concatenate([wide, jnp.zeros((4, 256), F32)], axis=0)
    r.wq[member] = wide.astype(BF)
    for load in loads[1:]:
        load.wait()

    perm = one_hot(128, 128, lambda i: (i % 8) * 16 + i // 8)
    t_rows = dot(perm, r.tok[...])
    c_rows = dot(perm, r.cot[...])
    r.send_rows[...] = jnp.concatenate(
        [t_rows.reshape(16, 8, 768), c_rows.reshape(16, 8, 768)], axis=1
    ).astype(BF)

    pl.semaphore_wait(barrier, 25)

    def quad(d):
        other = (member + d) % 4
        return other, at_k(((other // 2) + 2 * (x // 2)) * 2 + other % 2)

    for d in range(1, 4):
        other, dev = quad(d)
        go("q", r.wq.at[member], r.wq.at[member], d, member, dev)
    for d in range(1, 4):
        other, dev = quad(d)
        arrived("q", r.wq.at[other], other, dev)
    stack = one_hot(48, 64, lambda i: (i // 12) * 16 + i % 12)
    block = dot(stack, r.wq[...].reshape(64, 256)).astype(BF)
    r.wpart[0] = block[:, :128]
    r.wpart[1] = block[:, 128:]

    w_mine = r.wb.at[core, z_hi, y, z_lo // 2, j]

    @pl.when(holder)
    def _():
        w_mine[...] = r.wpart[core]

        @pl.loop(1, 16)
        def _(d):
            rcopy("wz", r.wpart.at[core], w_mine, d, z, at_z((z + d) % 16)).start()

    r.p1[z_lo, z_hi] = r.send_rows[z]

    @pl.loop(1, 16)
    def _(d):
        c = (z + d) % 16
        rcopy("p1", r.send_rows.at[c], r.p1.at[z_lo, z_hi], d, z, at_z(c)).start()

    @pl.loop(0, 8)
    def _(i):
        c = 2 * i + p

        @pl.when(c != z)
        def _():
            arrived("wz", r.wb.at[core, c // 8, y, (c % 8) // 2, j], c, at_z(c))

    def w_a(v):
        return r.wb.at[core, 0, y, :, j_of(v)]

    def w_b(v):
        return r.wb.at[core, 1, v, :, j]

    for d in range(1, 4):
        go("wa1", w_a(x), w_a(x), d, x, at_x((x + d) % 4))
        go("wb1", w_b(y), w_b(y), d, y, at_y((y + d) % 4))
    for d in range(1, 4):
        v = (x + d) % 4
        arrived("wa1", w_a(v), v, at_x(v))
    for d in range(1, 4):
        go("wa2", r.wb.at[core, 0, y], r.wb.at[core, 0, y], d, y, at_y((y + d) % 4))
    for d in range(1, 4):
        v = (y + d) % 4
        arrived("wb1", w_b(v), v, at_y(v))
    b_mine = r.wb.at[core, 1, :, :, j]
    for d in range(1, 4):
        go("wb2", b_mine, b_mine, d, x, at_x((x + d) % 4))
    go("wca", r.wb.at[core, 0, y], r.wb.at[core, 0, y], 0, y, pair)
    go("wcb", b_mine, b_mine, 0, x, pair)
    for d in (1, 3, 2):
        v = (y + d) % 4
        arrived("wa2", r.wb.at[core, 0, v], v, at_y(v))
        go("wca", r.wb.at[core, 0, v], r.wb.at[core, 0, v], d, v, pair)
        v = (x + d) % 4
        theirs = r.wb.at[core, 1, :, :, j_of(v)]
        arrived("wb2", theirs, v, at_x(v))
        go("wcb", theirs, theirs, d, v, pair)

    @pl.loop(1, 16)
    def _(d):
        c = (z + d) % 16
        arrived("p1", r.p1.at[c % 8, c // 8], c, at_z(c))

    for d in range(1, 4):
        v = (y + d) % 4
        go("xl", r.p1.at[pl.ds(2 * v, 2)], r.xb.at[:, y], d, y, at_y(v))
    r.xb[:, y] = r.p1[pl.ds(2 * y, 2)]
    perm_v = one_hot(
        256, 256, lambda i: (i % 8) * 32 + (i // 128) * 16 + ((i // 8) % 2) * 8 + (i // 16) % 8
    )
    r.zv[...] = dot(perm_v, r.p1[...].reshape(256, 768)).astype(BF).reshape(8, 2, 16, 768)
    for d in range(1, 8):
        v = (k + d) % 8
        go("zl", r.zv.at[v], r.zb.at[:, k], d, k, at_k(v))
    r.zb[:, k] = r.zv[k]

    for d in range(4):
        v = (y + d) % 4
        arrived("wca", r.wb.at[1 - core, 0, v], v, pair)
        v = (x + d) % 4
        arrived("wcb", r.wb.at[1 - core, 1, :, :, j_of(v)], v, pair)

    gain_row, bias_row = r.gain[...].reshape(1, 768), r.bias[...].reshape(1, 768)
    row_i = lax.broadcasted_iota(jnp.int32, (128, 128), 0)
    col_i = lax.broadcasted_iota(jnp.int32, (128, 128), 1)

    def home(idx, rows, same):
        here = slice(idx * 128, (idx + 1) * 128)
        f = rows.astype(F32)
        t = f[:, :8].reshape(128, 768)
        c16 = f[:, 8:].reshape(128, 768).astype(BF)
        centred = t - jnp.mean(t, axis=-1, keepdims=True)
        inv = lax.rsqrt(jnp.mean(centred * centred, axis=-1, keepdims=True) + EPS)
        nrm = centred * inv
        normed = (nrm * gain_row + bias_row).astype(BF)
        r.lt[0, :, here] = normed.T
        r.lt[1, :, here] = c16.T
        r.gn_acc[...] = jnp.zeros_like(r.gn_acc)

        @pl.loop(0, 2)
        def _(g):
            def w_of(part):
                blocks = [r.wb[part, g, v].reshape(768, 128) for v in range(4)]
                return jnp.concatenate(blocks, axis=1)

            def heads(proj):
                ones = [swap(proj[:, e:e + 128], proj[:, e + 128:e + 256]) for e in (0, 256)]
                return [
                    jnp.concatenate([ones[0][i], ones[1][i]], axis=1).astype(BF) for i in range(2)
                ]

            def blocks_of(a, b):
                pairs = [swap(a[:, e:e + 128], b[:, e:e + 128]) for e in (0, 128)]
                return jnp.concatenate([*pairs[0], *pairs[1]], axis=1).astype(BF)

            q, kk = heads(dot(normed, w_of(0)))
            low = lax.broadcasted_iota(jnp.int32, (128, 512), 1) % 128 < 64
            w_vu = w_of(1)
            vu = jnp.where(low, dot(normed, w_vu), dot(c16, w_vu))
            v, u = heads(vu)
            lane_head = lax.broadcasted_iota(jnp.int32, (128, 256), 1) // 64

            def spread(a):
                return jnp.concatenate(
                    [jnp.where(lane_head == h, a, jnp.zeros_like(a)) for h in range(4)], axis=0
                )

            qs, ks, vs, us = spread(q), spread(kk), spread(v), spread(u)
            s = dot_nt(q, ks)
            dp = dot_nt(u, vs)
            lows, dss = [], []
            for h in range(4):
                sj = jnp.where(same, s[:, h * 128:(h + 1) * 128] * SCALE, -1e30)
                e = jnp.exp(sj - jnp.max(sj, axis=-1, keepdims=True))
                pr = e / jnp.sum(e, axis=-1, keepdims=True)
                dpj = dp[:, h * 128:(h + 1) * 128]
                delta = jnp.sum(pr * dpj, axis=-1, keepdims=True)
                dss.append((pr * (dpj - delta) * SCALE).astype(BF))
                lows.append(pr.astype(BF))
            p_wide, ds_wide = jnp.concatenate(lows, axis=1), jnp.concatenate(dss, axis=1)
            p_tall, ds_tall = jnp.concatenate(lows, axis=0), jnp.concatenate(dss, axis=0)
            att = dot(p_wide, vs)
            gq = dot(ds_wide, ks)
            gk = dot_tn(ds_tall, qs)
            gv = dot_tn(p_tall, us)
            g_qk = blocks_of(gq, gk)
            r.gs_qk[g, here, :] = g_qk
            r.gs_v[g, here, :] = gv.astype(BF)
            r.gs_a[g, here, :] = att.astype(BF)
            g_v = blocks_of(gv, jnp.zeros_like(gv))
            r.gn_acc[...] += dot_nt(g_qk, w_of(0)) + dot_nt(g_v, w_vu)

        g = r.gn_acc[...]
        part = jnp.concatenate(
            [jnp.sum(g * nrm, axis=0, keepdims=True), jnp.sum(g, axis=0, keepdims=True)], axis=0
        )
        return g, nrm, inv, part

    g, nrm, inv, norm_part = home(0, r.send_rows[...], row_i % 8 == col_i % 8)
    r.gn_y[...] = g
    r.nrm_y[...] = nrm
    r.inv_y[...] = jnp.broadcast_to(inv, (128, 128))

    for d in range(1, 4):
        v = (y + d) % 4
        arrived("xl", r.xb.at[:, v], v, at_y(v))
    half = row_i // 64 == col_i // 64
    g, _, _, part = home(1, r.xb[...].reshape(16, 16, 768), half)
    norm_part = norm_part + part
    r.gx[...] = g.astype(BF).reshape(2, 4, 16, 768)
    for d in range(1, 4):
        v = (y + d) % 4
        go("gx", r.gx.at[:, v], r.xg.at[pl.ds(2 * y, 2)], d, y, at_y(v))
    r.xg[pl.ds(2 * y, 2)] = r.gx[:, y]

    for d in range(1, 8):
        v = (k + d) % 8
        arrived("zl", r.zb.at[:, v], v, at_k(v))
    g, _, _, part = home(2, r.zb[...].reshape(16, 16, 768), half)
    norm_part = norm_part + part
    g4 = g.reshape(2, 8, 8, 768)
    r.gz[...] = jnp.concatenate([g4[0], g4[1]], axis=1).astype(BF)
    for d in range(1, 8):
        v = (k + d) % 8
        go("gz", r.gz.at[v], r.zg.at[k], d, k, at_k(v))
    r.zg[k] = r.gz[k]

    r.nc[core] = norm_part
    go("nc", r.nc.at[core], r.nc.at[core], 0, core, pair)

    def weight_grad(part, g, dest):
        lhs = r.lt[0]
        if part == 0:
            full = dot(lhs, r.gs_qk[g])
            blocks = [full[:, e:e + 128] for e in range(0, 512, 128)]
        else:
            gv, ga = dot(lhs, r.gs_v[g]), dot(r.lt[1], r.gs_a[g])
            blocks = []
            for e in (0, 128):
                blocks.extend(swap(gv[:, e:e + 128], ga[:, e:e + 128]))
        for v in range(4):
            dest[g, v] = blocks[v].astype(dest.dtype)

    for g in range(2):
        for part in range(2):
            @pl.when(core == 1 - part)
            def _():
                weight_grad(part, g, r.gw_send)
        go("c", r.gw_send.at[g], r.gw_recv.at[g], g, g, pair)
    for g in range(2):
        for part in range(2):
            @pl.when(core == part)
            def _():
                weight_grad(part, g, r.gw_own)

    for d in range(1, 4):
        v = (y + d) % 4
        arrived("gx", r.xg.at[pl.ds(2 * v, 2)], v, at_y(v))
    for d in range(1, 8):
        v = (k + d) % 8
        arrived("gz", r.zg.at[v], v, at_k(v))
    perm_g = one_hot(128, 128, lambda i: (i % 16) * 8 + i // 16)
    total = dot(perm_g, r.zg[...].reshape(128, 768)) + r.xg[...].reshape(128, 768).astype(F32)
    total = total.reshape(16, 8, 768)
    total = jnp.concatenate([total[:, :, :384], total[:, :, 384:]], axis=1).astype(BF)
    r.rb[...] = total.reshape(8, 2, 16, 384)

    @pl.loop(1, 16)
    def _(d):
        c = (z + d) % 16
        rcopy("rt", r.rb.at[c % 8, c // 8], r.ret.at[z], d, z, at_z(c)).start()

    r.ret[z] = r.rb[z_lo, z_hi]

    arrived("nc", r.nc.at[1 - core], 1 - core, pair)
    r.ny[y] = r.nc[0] + r.nc[1]
    for d in range(1, 4):
        go("ny", r.ny.at[y], r.ny.at[y], d, y, at_y((y + d) % 4))

    arrived("c", r.gw_recv.at[0], 0, pair)
    for d in (2, 1, 3, 0):
        v = (y + d) % 4
        r.a1s[v] = (r.gw_own[0, v] + r.gw_recv[0, v].astype(F32)).astype(BF)
        if d:
            go("a1", r.a1s.at[v], r.a1r.at[y], d, y, at_y(v))
    r.a1r[y] = r.a1s[y]
    arrived("c", r.gw_recv.at[1], 1, pair)
    both = (r.gw_own[1] + r.gw_recv[1].astype(F32)).astype(BF).reshape(4, 4, 4, 48, 128)
    for e in range(4):
        r.b1s[e] = both[:, :, e]
    for d in (2, 1, 3):
        v = (x + d) % 4
        go("b1", r.b1s.at[j_of(v)], r.b1r.at[x], d, x, at_x(v))
    r.b1r[x] = r.b1s[j]

    for d in range(1, 4):
        v = (y + d) % 4
        arrived("ny", r.ny.at[v], v, at_y(v))
    r.nx[x] = (r.ny[0] + r.ny[1]) + (r.ny[2] + r.ny[3])
    for d in range(1, 4):
        go("nx", r.nx.at[x], r.nx.at[x], d, x, at_x((x + d) % 4))

    def four(ref):
        return (ref[0].astype(F32) + ref[1].astype(F32)) + (ref[2].astype(F32) + ref[3].astype(F32))

    for d in range(1, 4):
        v = (y + d) % 4
        arrived("a1", r.a1r.at[v], v, at_y(v))
    a_sum = four(r.a1r).astype(BF).reshape(4, 4, 48, 128)
    for e in range(4):
        r.a2s[e] = a_sum[:, e]
    for d in (2, 1, 3):
        v = (x + d) % 4
        go("a2", r.a2s.at[j_of(v)], r.a2r.at[x], d, x, at_x(v))
    r.a2r[x] = r.a2s[j]
    for d in range(1, 4):
        v = (x + d) % 4
        arrived("b1", r.b1r.at[v], v, at_x(v))
    r.b2s[...] = four(r.b1r).astype(BF)
    for d in (2, 1, 3):
        v = (y + d) % 4
        go("b2", r.b2s.at[v], r.b2r.at[y], d, y, at_y(v))
    r.b2r[y] = r.b2s[y]

    for d in range(1, 4):
        v = (x + d) % 4
        arrived("nx", r.nx.at[v], v, at_x(v))
    r.nz[z] = (r.nx[0] + r.nx[1]) + (r.nx[2] + r.nx[3])

    @pl.loop(1, 16)
    def _(d):
        c = (z + d) % 16
        rcopy("nz", r.nz.at[z], r.nz.at[z], d, z, at_z(c)).start()

    for d in range(1, 4):
        v = (x + d) % 4
        arrived("a2", r.a2r.at[v], v, at_x(v))
    r.zs[0] = four(r.a2r).astype(BF)
    for d in range(1, 4):
        v = (y + d) % 4
        arrived("b2", r.b2r.at[v], v, at_y(v))
    r.zs[1] = four(r.b2r).astype(BF)

    def z_copy(i):
        c = 2 * i + p
        return rcopy("z", r.zs.at[c // 8, (c % 8) // 2], r.zr.at[z], i, z, at_z(c))

    @pl.loop(0, 8)
    def _(i):
        @pl.when(2 * i + p != z)
        def _():
            z_copy(i).start()

    @pl.when(holder)
    def _():
        r.zr[z] = r.zs[z_hi, z_lo // 2]

    @pl.loop(1, 16)
    def _(d):
        c = (z + d) % 16
        arrived("rt", r.ret.at[c], c, at_z(c))

    back = r.ret[...].astype(F32)
    back = jnp.concatenate([back[:, :8], back[:, 8:]], axis=2).reshape(128, 768)
    scaled = (r.gn_y[...] + back) * gain_row
    nrm = r.nrm_y[...]
    m1 = jnp.mean(scaled, axis=-1, keepdims=True)
    m2 = jnp.mean(scaled * nrm, axis=-1, keepdims=True)
    c_rows = r.send_rows[...].astype(F32)[:, 8:].reshape(128, 768)
    rows = (c_rows + r.inv_y[:, :1] * (scaled - m1 - nrm * m2)).astype(BF)
    perm_b = one_hot(128, 128, lambda i: (i % 16) * 8 + i // 16)
    r.tok_out[...] = dot(perm_b, rows).astype(BF)
    store_tok = pltpu.make_async_copy(r.tok_out, tok_res, lsem.at[5])
    store_tok.start()

    @pl.loop(1, 16)
    def _(d):
        c = (z + d) % 16
        arrived("nz", r.nz.at[c], c, at_z(c))

    norm_total = r.nz[0]
    for c in range(1, 16):
        norm_total = norm_total + r.nz[c]
    r.norm_out[...] = norm_total
    store_norm = pltpu.make_async_copy(r.norm_out, norm_res, lsem.at[6])
    store_norm.start()

    def final_copies():
        return [rcopy("f", r.qr.at[core], r.qr.at[core], d, core, quad(d)[1]) for d in range(1, 4)]

    @pl.when(holder)
    def _():
        @pl.loop(1, 16)
        def _(d):
            c = (z + d) % 16
            arrived("z", r.zr.at[c], c, at_z(c))

        z_total = r.zr[0].astype(F32)
        for c in range(1, 16):
            z_total = z_total + r.zr[c].astype(F32)
        r.qr[core] = z_total
        for copy in final_copies():
            copy.start()
        arrived("f", r.qr.at[1 - core], 1 - core, pair)

    @pl.when(jnp.logical_not(holder))
    def _():
        for d in range(2):
            arrived("f", r.qr.at[d], d, at_k((x + 1 - 2 * p) * 2 + d))

    store_w = pltpu.make_async_copy(r.qr, w_res, lsem.at[7])
    store_w.start()

    for copy in sends:
        copy.wait_send()

    @pl.loop(1, 16)
    def _(d):
        c = (z + d) % 16
        dev = at_z(c)
        rcopy("p1", r.send_rows.at[c], r.p1.at[z_lo, z_hi], d, z, dev).wait_send()
        rcopy("rt", r.rb.at[c % 8, c // 8], r.ret.at[z], d, z, dev).wait_send()
        rcopy("nz", r.nz.at[z], r.nz.at[z], d, z, dev).wait_send()

    @pl.loop(0, 8)
    def _(i):
        @pl.when(2 * i + p != z)
        def _():
            z_copy(i).wait_send()

    @pl.when(holder)
    def _():
        @pl.loop(1, 16)
        def _(d):
            rcopy("wz", r.wpart.at[core], w_mine, d, z, at_z((z + d) % 16)).wait_send()

        for copy in final_copies():
            copy.wait_send()

    store_tok.wait()
    store_norm.wait()
    store_w.wait()


def per_device(tokens, cotangent, weights, norm_gain, norm_bias):
    scratch = list(BUFFERS.values())
    for count in SEMAPHORES.values():
        scratch += [pltpu.SemaphoreType.DMA((count,))] * 2
    scratch.append(pltpu.SemaphoreType.DMA((8,)))
    anywhere = pl.BlockSpec(memory_space=pl.ANY)
    grad_tok, grad_w, grad_norm = pl.pallas_call(
        kernel,
        out_shape=(
            jax.ShapeDtypeStruct((128, 768), BF),
            jax.ShapeDtypeStruct((2, 48, 128), F32),
            jax.ShapeDtypeStruct((2, 768), F32),
        ),
        in_specs=[anywhere] * 5,
        out_specs=(anywhere,) * 3,
        scratch_shapes=scratch,
        compiler_params=pltpu.CompilerParams(
            collective_id=0, has_side_effects=True, vmem_limit_bytes=52 * 1024 * 1024
        ),
        name="axial_backward",
    )(tokens.reshape(128, 768), cotangent.reshape(128, 768), weights, norm_gain, norm_bias)
    member = lax.axis_index("slab") % 4
    mine = lax.dynamic_slice(grad_w, (0, member * 12, 0), (2, 12, 128))
    mine = mine.reshape(2, 12, 2, 64).transpose(1, 0, 2, 3).reshape(12, 4, 64)
    return grad_tok.reshape(tokens.shape), mine, grad_norm


def solution(mesh):
    return jax.shard_map(
        per_device,
        mesh=mesh,
        in_specs=(
            P("slab", "head", None, None),
            P("slab", "head", None, None),
            P("slab", None, "head"),
            P(),
            P(),
        ),
        out_specs=(P("slab", "head", None, None), P("slab", None, "head"), P()),
        check_vma=False,
    )
```

time: 1370 us -> 105 us (0.08)
  waiting for transfers between devices: 1010 us -> 0 us
  blocking collectives: 256 us -> 0 us
  Pallas kernels: 0 us -> 98.9 us
  local copies, waits for them, and re-layouts: 33.6 us -> 4.53 us
  matrix products: 25.1 us -> 0 us
  starting transfers between devices: 22.5 us -> 0 us
  between operations: 14.9 us -> 0.7 us
    unnamed x5 -> x0, waiting for transfers between devices: 825 us -> none
    all_gather x1 -> x0, blocking collectives: 151 us -> none  [per_device(): local_w = lax.all_gather(weights, 'slab', axis=0, tiled=True)]
    all_to_all x3 -> x0, waiting for transfers between devices: 128 us -> none  [the longest x1 87 us: depth_attention(): lax.all_to_all(returned, 'slab', split_axis=0, concat_axis=1, tiled=True)]
    psum x1 -> x0, blocking collectives: 105 us -> none  [per_device(): gain_sum, bias_sum = lax.psum((gain_part, bias_part), ('slab', 'head'))]
    pallas_call x0 -> x1, Pallas kernels: none -> 98.9 us  [per_device(): pl.pallas_call(kernel, out_shape=(jax.ShapeDtypeStruct((128, 768), BF), j...]
    all_gather x3 -> x0, waiting for transfers between devices: 55.3 us -> none  [the longest x1 55.2 us: per_device(): lax.all_gather(normed, 'head', axis=1, tiled=True)]
    dot_general x19 -> x0, matrix products: 23.2 us -> none  [the longest x3 4.06 us: line_grads(): jnp.einsum('bglm,blgd->bmgd', dscores, q_lines, preferred_element_type=jn...]
    all_to_all x3 -> x0, starting transfers between devices: 21.9 us -> none  [the longest x1 7.78 us: per_device(): lax.all_to_all(packed, 'slab', split_axis=1, concat_axis=0, tiled=True)]
  transfers between devices with their start and end apart: 7 -> 0, of which waited for: 4 -> 0; matrix products, arithmetic and copies ran while one was open for 4% -> 0% of each run, Pallas kernels for 0% -> 0%
where the time goes in v2:
time: 105 us; the launch traced here: 104 us
  Pallas kernels  98.9 us (94%)
  local copies, waits for them, and re-layouts  4.53 us (4%)
    pallas_call x1, Pallas kernels, per_device(): pl.pallas_call(kernel, out_shape=(jax.ShapeDtypeStruct((128, 768), BF), j...  98.9 us
    unnamed x12, local copies, waits for them, and re-layouts  3.81 us

profile of v2, /device:TPU:1, one launch (start us, length us, event | category | flops | bytes accessed | tf_op | source)
XLA Modules:
  0.0 104.1 jit_solution(9301701434564122926)
XLA Ops:
  0.6 0.0 copy-start.2
  0.7 0.0 copy-start.4
  0.7 0.0 copy-start.3
  0.7 0.7 copy-done.2
  1.3 0.0 copy-done.4
  1.3 0.0 copy-done.3
  1.4 0.0 copy-start
  1.4 0.9 copy-done
  2.3 0.0 copy-start.1
  2.3 0.9 copy-done.1
  3.2 98.9 %axial_backward.1 = (bf16[128,768]{1,0:T(8,128)(2,1)S(1)}, f32[2,48,128]{2,1,0:T(8,128)S(1)}, f32[2,768]{1,0:T(2,128)S(1)}) custom-call(bf16[128,768]{1,0:T(8,128)(2,1)S(1)} %bitcast.8, bf16[128,768]{1,0:T(8,128)(2,1)S(1)} %bitcast.9, bf16[12,4,64]{2,1,0:T(4,128)(2,1)S(1)} %copy-done.2, f32[768]{0:T(1024)S(1)} %copy-done.3, f32[768]{0:T(1024)S(1)} %copy-done.4), custom_call_target="tpu_custom_call" | custom-call | tf_op jit(solution)/shard_map/axial_backward/pallas_call | solution.py:608
  102.2 0.7 reshape.24
  102.9 0.7 copy.11
  103.5 0.6 copy.12
  (2 shorter events, 0.0 us)
Async XLA Ops:
  0.6 0.7 copy-start.2
  0.7 0.7 copy-start.4
  0.7 0.7 copy-start.3
  1.4 0.9 copy-start
  2.3 0.9 copy-start.1

commit v3 on v2

v3 whole, which is shorter than its diff:
```python
import types

import jax
import jax.numpy as jnp
from jax import lax
from jax.experimental import pallas as pl
from jax.experimental.pallas import tpu as pltpu
from jax.sharding import PartitionSpec as P

MESH = pl.DeviceIdType.MESH
BF = jnp.bfloat16
F32 = jnp.float32
EPS = 1e-05
SCALE = 0.125
VM = pltpu.VMEM

BUFFERS = {
    "tok": VM((128, 768), BF),
    "cot": VM((128, 768), BF),
    "wraw": VM((12, 4, 64), BF),
    "gain": VM((768,), F32),
    "bias": VM((768,), F32),
    "wq": VM((4, 16, 256), BF),
    "wpart": VM((2, 48, 128), BF),
    "wb": VM((2, 2, 4, 4, 4, 48, 128), BF),
    "wsep": VM((4, 2, 768, 256), BF),
    "send_rows": VM((2, 16, 16, 384), BF),
    "p1": VM((2, 8, 2, 16, 384), BF),
    "xb": VM((2, 2, 4, 2, 16, 384), BF),
    "zv": VM((2, 8, 2, 16, 384), BF),
    "zb": VM((2, 2, 8, 16, 384), BF),
    "lt": VM((2, 768, 384), BF),
    "normed": VM((3, 128, 768), BF),
    "c16": VM((3, 128, 768), BF),
    "nrm": VM((3, 128, 768), F32),
    "gn": VM((3, 128, 768), F32),
    "gs_qk": VM((2, 384, 512), BF),
    "gs_v": VM((2, 384, 256), BF),
    "gs_a": VM((2, 384, 256), BF),
    "inv_y": VM((128, 128), F32),
    "gx": VM((2, 4, 16, 768), BF),
    "xg": VM((8, 16, 768), BF),
    "gz": VM((8, 16, 768), BF),
    "zg": VM((8, 16, 768), BF),
    "rb": VM((8, 2, 16, 384), BF),
    "ret": VM((16, 16, 384), BF),
    "gw_send": VM((2, 4, 768, 128), BF),
    "gw_recv": VM((2, 4, 768, 128), BF),
    "gw_own": VM((2, 4, 768, 128), F32),
    "a1s": VM((2, 4, 2, 4, 48, 128), BF),
    "a1r": VM((2, 4, 2, 4, 48, 128), BF),
    "b1s": VM((2, 4, 4, 2, 48, 128), BF),
    "b1r": VM((2, 4, 4, 2, 48, 128), BF),
    "a2s": VM((2, 4, 2, 48, 128), BF),
    "a2r": VM((2, 4, 2, 48, 128), BF),
    "b2s": VM((2, 4, 2, 48, 128), BF),
    "b2r": VM((2, 4, 2, 48, 128), BF),
    "zs": VM((2, 4, 48, 128), BF),
    "zr": VM((16, 48, 128), BF),
    "qr": VM((2, 48, 128), F32),
    "tok_out": VM((128, 768), BF),
    "norm_out": VM((2, 1, 768), F32),
    "nk": VM((8, 2, 768), F32),
    "ny": VM((4, 1, 768), F32),
    "nz": VM((16, 1, 768), F32),
}
SEMAPHORES = {
    "q": 4, "wz": 16, "wa1": 4, "wb1": 4, "wa2": 4, "wb2": 4, "wca": 4, "wcb": 4,
    "p1": 32, "xl": 8, "zl": 16, "gx": 4, "gz": 8, "rt": 16,
    "c": 2, "a1": 8, "b1": 8, "a2": 8, "b2": 8, "z": 16, "f": 4,
    "nk": 8, "ny": 4, "nz": 16, "no": 2,
}


def one_hot(rows, cols, source):
    dest = lax.broadcasted_iota(jnp.int32, (rows, cols), 0)
    src = lax.broadcasted_iota(jnp.int32, (rows, cols), 1)
    return (source(dest) == src).astype(BF)


def dot(a, b):
    return jnp.dot(a, b, preferred_element_type=F32)


def dot_nt(a, b):
    return lax.dot_general(a, b, (((1,), (1,)), ((), ())), preferred_element_type=F32)


def dot_tn(a, b):
    return lax.dot_general(a, b, (((0,), (0,)), ((), ())), preferred_element_type=F32)


def fold(a):
    return jnp.concatenate([a[:, :, :384], a[:, :, 384:]], axis=1)


def unfold(a):
    a = a.astype(F32)
    return jnp.concatenate([a[:, :8], a[:, 8:]], axis=2).reshape(-1, 768)


def swap(a, b):
    low = lax.broadcasted_iota(jnp.int32, a.shape, 1) < 64
    return jnp.where(low, a, pltpu.roll(b, 64, 1)), jnp.where(low, pltpu.roll(a, 64, 1), b)


def kernel(tok_in, cot_in, w_in, gain_in, bias_in, tok_res, w_res, norm_res, *refs):
    names = list(BUFFERS)
    r = types.SimpleNamespace(**dict(zip(names, refs)))
    rest = refs[len(names):]
    ssem = {n: rest[2 * i] for i, n in enumerate(SEMAPHORES)}
    rsem = {n: rest[2 * i + 1] for i, n in enumerate(SEMAPHORES)}
    lsem = rest[-1]

    slab = lax.axis_index("slab")
    head = lax.axis_index("head")
    z_lo, x, core = slab // 8, (slab // 2) % 4, slab % 2
    y, z_hi = head // 2, head % 2
    z = z_hi * 8 + z_lo
    k = x * 2 + core
    p = x % 2
    j = 2 * p + x // 2
    member = p * 2 + core
    holder = z_lo % 2 == p

    def at_z(c):
        return ((c % 8) * 8 + k, y * 2 + c // 8)

    def at_y(v):
        return (slab, v * 2 + z_hi)

    def at_k(v):
        return (z_lo * 8 + v, head)

    def at_x(v):
        return at_k(v * 2 + core)

    def j_of(v):
        return 2 * (v % 2) + v // 2

    pair = at_k(x * 2 + 1 - core)

    def rcopy(name, src, dst, si, ri, dev):
        return pltpu.make_async_remote_copy(
            src_ref=src, dst_ref=dst, send_sem=ssem[name].at[si], recv_sem=rsem[name].at[ri],
            device_id=dev, device_id_type=MESH,
        )

    sends = []

    def go(*args):
        copy = rcopy(*args)
        copy.start()
        sends.append(copy)

    def arrived(name, dst, ri, dev):
        rcopy(name, dst, dst, 0, ri, dev).wait_recv()

    loads = [
        pltpu.make_async_copy(src, dst, lsem.at[i])
        for i, (src, dst) in enumerate(
            ((w_in, r.wraw), (tok_in, r.tok), (cot_in, r.cot), (gain_in, r.gain), (bias_in, r.bias))
        )
    ]
    for load in loads:
        load.start()

    barrier = pltpu.get_barrier_semaphore()

    @pl.loop(1, 16)
    def _(d):
        pl.semaphore_signal(barrier, inc=1, device_id=at_z((z + d) % 16), device_id_type=MESH)

    for d in range(1, 4):
        pl.semaphore_signal(barrier, inc=1, device_id=at_y((y + d) % 4), device_id_type=MESH)
    for d in range(1, 8):
        pl.semaphore_signal(barrier, inc=1, device_id=at_k((k + d) % 8), device_id_type=MESH)

    loads[0].wait()
    wide = jnp.concatenate([r.wraw[:, c, :].astype(F32) for c in range(4)], axis=1)
    wide = jnp.concatenate([wide, jnp.zeros((4, 256), F32)], axis=0)
    r.wq[member] = wide.astype(BF)
    pl.semaphore_wait(barrier, 25)

    def quad(d):
        other = (member + d) % 4
        return other, at_k(((other // 2) + 2 * (x // 2)) * 2 + other % 2)

    for d in range(1, 4):
        other, dev = quad(d)
        go("q", r.wq.at[member], r.wq.at[member], d, member, dev)

    for load in loads[1:]:
        load.wait()

    perm = one_hot(128, 128, lambda i: (i % 8) * 16 + i // 8)
    for e, ref in enumerate((r.tok, r.cot)):
        r.send_rows[e] = fold(dot(perm, ref[...]).reshape(16, 8, 768)).astype(BF)

    def token_copy(e, d):
        c = (z + d) % 16
        return rcopy("p1", r.send_rows.at[e, c], r.p1.at[e, z_lo, z_hi], 16 * e + d, 16 * e + z, at_z(c))

    def token_sends(e, start, stop):
        @pl.loop(start, stop)
        def _(i):
            token_copy(e, 8 + (1 - 2 * (i % 2)) * ((i + 1) // 2)).start()

    gain_row, bias_row = r.gain[...].reshape(1, 768), r.bias[...].reshape(1, 768)

    def prepare_cotangent(idx, rows):
        c16 = unfold(rows).astype(BF)
        r.lt[1, :, idx * 128:(idx + 1) * 128] = c16.T
        r.c16[idx] = c16

    def prepare(idx, rows):
        here = slice(idx * 128, (idx + 1) * 128)
        t = unfold(rows)
        centred = t - jnp.mean(t, axis=-1, keepdims=True)
        inv = lax.rsqrt(jnp.mean(centred * centred, axis=-1, keepdims=True) + EPS)
        nrm = centred * inv
        normed = (nrm * gain_row + bias_row).astype(BF)
        r.lt[0, :, here] = normed.T
        r.normed[idx] = normed
        r.nrm[idx] = nrm
        r.gn[idx] = jnp.zeros((128, 768), F32)
        return inv

    for d in range(1, 4):
        other, dev = quad(d)
        arrived("q", r.wq.at[other], other, dev)
    stack = one_hot(48, 64, lambda i: (i // 12) * 16 + i % 12)
    block = dot(stack, r.wq[...].reshape(64, 256)).astype(BF)
    r.wpart[0] = block[:, :128]
    r.wpart[1] = block[:, 128:]

    w_mine = r.wb.at[core, z_hi, y, z_lo // 2, j]

    @pl.when(holder)
    def _():
        w_mine[...] = r.wpart[core]

        @pl.loop(1, 16)
        def _(d):
            rcopy("wz", r.wpart.at[core], w_mine, d, z, at_z((z + d) % 16)).start()

    r.inv_y[...] = jnp.broadcast_to(prepare(0, r.send_rows[0]), (128, 128))
    prepare_cotangent(0, r.send_rows[1])

    @pl.loop(0, 8)
    def _(i):
        c = 2 * i + p

        @pl.when(c != z)
        def _():
            arrived("wz", r.wb.at[core, c // 8, y, (c % 8) // 2, j], c, at_z(c))

    def w_a(v):
        return r.wb.at[core, 0, y, :, j_of(v)]

    def w_b(v):
        return r.wb.at[core, 1, v, :, j]

    for d in range(1, 4):
        go("wa1", w_a(x), w_a(x), d, x, at_x((x + d) % 4))
        go("wb1", w_b(y), w_b(y), d, y, at_y((y + d) % 4))
    token_sends(0, 0, 8)
    for e in range(2):
        r.p1[e, z_lo, z_hi] = r.send_rows[e, z]

    for d in range(1, 4):
        v = (x + d) % 4
        arrived("wa1", w_a(v), v, at_x(v))
    a_mine, b_mine = r.wb.at[core, 0, y], r.wb.at[core, 1, :, :, j]
    go("wca", a_mine, a_mine, 0, y, pair)
    for d, span in ((1, (8, 10)), (3, (10, 12)), (2, (12, 15))):
        go("wa2", a_mine, a_mine, d, y, at_y((y + d) % 4))
        token_sends(0, *span)
    for d in range(1, 4):
        v = (y + d) % 4
        arrived("wb1", w_b(v), v, at_y(v))
    go("wcb", b_mine, b_mine, 0, x, pair)
    for d, span in ((1, (0, 4)), (3, (4, 8)), (2, (8, 15))):
        go("wb2", b_mine, b_mine, d, x, at_x((x + d) % 4))
        token_sends(1, *span)

    perm_v = one_hot(
        256, 256, lambda i: (i % 8) * 32 + (i // 128) * 16 + ((i // 8) % 2) * 8 + (i // 16) % 8
    )

    def second_hop(e):
        @pl.loop(1, 16)
        def _(d):
            c = (z + d) % 16
            arrived("p1", r.p1.at[e, c % 8, c // 8], 16 * e + c, at_z(c))

        for d in range(1, 4):
            v = (y + d) % 4
            go("xl", r.p1.at[e, pl.ds(2 * v, 2)], r.xb.at[e, :, y], 4 * e + d, 4 * e + y, at_y(v))
        r.xb[e, :, y] = r.p1[e, pl.ds(2 * y, 2)]
        r.zv[e] = dot(perm_v, r.p1[e].reshape(256, 384)).astype(BF).reshape(8, 2, 16, 384)
        for d in range(1, 8):
            v = (k + d) % 8
            go("zl", r.zv.at[e, v], r.zb.at[e, :, k], 8 * e + d, 8 * e + k, at_k(v))
        r.zb[e, :, k] = r.zv[e, k]

    def lines_arrived(e):
        for d in range(1, 4):
            v = (y + d) % 4
            arrived("xl", r.xb.at[e, :, v], 4 * e + v, at_y(v))
        for d in range(1, 8):
            v = (k + d) % 8
            arrived("zl", r.zb.at[e, :, v], 8 * e + v, at_k(v))

    second_hop(0)

    for d in (1, 3, 2):
        v = (y + d) % 4
        theirs = r.wb.at[core, 0, v]
        arrived("wa2", theirs, v, at_y(v))
        go("wca", theirs, theirs, d, v, pair)
        v = (x + d) % 4
        theirs = r.wb.at[core, 1, :, :, j_of(v)]
        arrived("wb2", theirs, v, at_x(v))
        go("wcb", theirs, theirs, d, v, pair)
    second_hop(1)

    for d in range(4):
        v = (y + d) % 4
        arrived("wca", r.wb.at[1 - core, 0, v], v, pair)
        v = (x + d) % 4
        arrived("wcb", r.wb.at[1 - core, 1, :, :, j_of(v)], v, pair)

    row_i = lax.broadcasted_iota(jnp.int32, (128, 128), 0)
    col_i = lax.broadcasted_iota(jnp.int32, (128, 128), 1)

    @pl.loop(0, 4)
    def _(i):
        part, g = i // 2, i % 2
        for e in range(2):
            both = [r.wb[part, g, 2 * e + h].reshape(768, 128).astype(F32) for h in range(2)]
            for h, block in enumerate(swap(*both)):
                r.wsep[2 * part + h, g, :, e * 128:(e + 1) * 128] = block.astype(BF)

    def lines(q, kk, v, u, same):
        lane_head = lax.broadcasted_iota(jnp.int32, (128, 256), 1) // 64

        def spread(a):
            return jnp.concatenate(
                [jnp.where(lane_head == h, a, jnp.zeros_like(a)) for h in range(4)], axis=0
            )

        qs, ks, vs, us = spread(q), spread(kk), spread(v), spread(u)
        s = dot_nt(q, ks)
        dp = dot_nt(u, vs)
        lows, dss = [], []
        for h in range(4):
            sj = jnp.where(same, s[:, h * 128:(h + 1) * 128] * SCALE, -1e30)
            e = jnp.exp(sj - jnp.max(sj, axis=-1, keepdims=True))
            pr = e / jnp.sum(e, axis=-1, keepdims=True)
            dpj = dp[:, h * 128:(h + 1) * 128]
            delta = jnp.sum(pr * dpj, axis=-1, keepdims=True)
            dss.append((pr * (dpj - delta) * SCALE).astype(BF))
            lows.append(pr.astype(BF))
        p_wide, ds_wide = jnp.concatenate(lows, axis=1), jnp.concatenate(dss, axis=1)
        p_tall, ds_tall = jnp.concatenate(lows, axis=0), jnp.concatenate(dss, axis=0)
        return dot(ds_wide, ks), dot_tn(ds_tall, qs), dot_tn(p_tall, us), dot(p_wide, vs)

    def blocks_of(a, b):
        pairs = [swap(a[:, e:e + 128], b[:, e:e + 128]) for e in (0, 128)]
        return jnp.concatenate([*pairs[0], *pairs[1]], axis=1).astype(BF)

    def home(first, count, g, same):
        normed = r.normed[first:first + count].reshape(count * 128, 768)
        c16 = r.c16[first:first + count].reshape(count * 128, 768)
        feats = [dot(normed, r.wsep[c, g]).astype(BF) for c in range(3)]
        feats.append(dot(c16, r.wsep[3, g]).astype(BF))
        grads = [[], [], []]
        for i in range(count):
            here = slice(i * 128, (i + 1) * 128)
            there = slice((first + i) * 128, (first + i + 1) * 128)
            gq, gk, gv, att = lines(*[a[here] for a in feats], same)
            r.gs_qk[g, there, :] = blocks_of(gq, gk)
            r.gs_v[g, there, :] = gv.astype(BF)
            r.gs_a[g, there, :] = att.astype(BF)
            for c, one in enumerate((gq, gk, gv)):
                grads[c].append(one.astype(BF))
        back = [dot_nt(jnp.concatenate(grads[c], axis=0), r.wsep[c, g]) for c in range(3)]
        back = (back[0] + back[1]) + back[2]
        for i in range(count):
            r.gn[first + i] += back[i * 128:(i + 1) * 128]

    @pl.loop(0, 2)
    def _(g):
        home(0, 1, g, row_i % 8 == col_i % 8)

    half = row_i // 64 == col_i // 64
    lines_arrived(0)
    prepare(1, r.xb[0].reshape(16, 16, 384))
    prepare(2, r.zb[0].reshape(16, 16, 384))
    lines_arrived(1)
    prepare_cotangent(1, r.xb[1].reshape(16, 16, 384))
    prepare_cotangent(2, r.zb[1].reshape(16, 16, 384))

    home(1, 2, 0, half)

    def weight_grad(part, g, dest):
        lhs = r.lt[0]
        if part == 0:
            full = dot(lhs, r.gs_qk[g])
            blocks = [full[:, e:e + 128] for e in range(0, 512, 128)]
        else:
            gv, ga = dot(lhs, r.gs_v[g]), dot(r.lt[1], r.gs_a[g])
            blocks = []
            for e in (0, 128):
                blocks.extend(swap(gv[:, e:e + 128], ga[:, e:e + 128]))
        for v in range(4):
            dest[g, v] = blocks[v].astype(dest.dtype)

    def to_other_core(g):
        for part in range(2):
            @pl.when(core == 1 - part)
            def _():
                weight_grad(part, g, r.gw_send)
        go("c", r.gw_send.at[g], r.gw_recv.at[g], g, g, pair)

    def own_part(g):
        for part in range(2):
            @pl.when(core == part)
            def _():
                weight_grad(part, g, r.gw_own)

    def four(ref):
        return (ref[0].astype(F32) + ref[1].astype(F32)) + (ref[2].astype(F32) + ref[3].astype(F32))

    def sum_first(g, between=lambda i: None):
        arrived("c", r.gw_recv.at[g], g, pair)
        for v in range(4):
            both = (r.gw_own[g, v] + r.gw_recv[g, v].astype(F32)).astype(BF).reshape(4, 4, 48, 128)
            r.a1s[g, v] = both[:2]
            for e in range(4):
                r.b1s[g, e, v] = both[2:, e]
        for i, d in enumerate((2, 1, 3)):
            between(i)
            v = (y + d) % 4
            go("a1", r.a1s.at[g, v], r.a1r.at[g, y], 4 * g + d, 4 * g + y, at_y(v))
            v = (x + d) % 4
            go("b1", r.b1s.at[g, j_of(v)], r.b1r.at[g, x], 4 * g + d, 4 * g + x, at_x(v))
        r.a1r[g, y] = r.a1s[g, y]
        r.b1r[g, x] = r.b1s[g, j]

    def sum_second(g):
        for d in range(1, 4):
            v = (y + d) % 4
            arrived("a1", r.a1r.at[g, v], 4 * g + v, at_y(v))
        a_sum = four(r.a1r.at[g]).astype(BF)
        for e in range(4):
            r.a2s[g, e] = a_sum[:, e]
        for d in (2, 1, 3):
            v = (x + d) % 4
            go("a2", r.a2s.at[g, j_of(v)], r.a2r.at[g, x], 4 * g + d, 4 * g + x, at_x(v))
        r.a2r[g, x] = r.a2s[g, j]
        for d in range(1, 4):
            v = (x + d) % 4
            arrived("b1", r.b1r.at[g, v], 4 * g + v, at_x(v))
        r.b2s[g] = four(r.b1r.at[g]).astype(BF)
        for d in (2, 1, 3):
            v = (y + d) % 4
            go("b2", r.b2s.at[g, v], r.b2r.at[g, y], 4 * g + d, 4 * g + y, at_y(v))
        r.b2r[g, y] = r.b2s[g, y]

    def z_copy(g, i):
        c = 8 * g + 2 * i + p
        return rcopy("z", r.zs.at[g, i], r.zr.at[z], 4 * g + i, z, at_z(c))

    def sum_third(g):
        for d in range(1, 4):
            v = (x + d) % 4
            arrived("a2", r.a2r.at[g, v], 4 * g + v, at_x(v))
        r.zs[g, 0:2] = four(r.a2r.at[g]).astype(BF)
        for d in range(1, 4):
            v = (y + d) % 4
            arrived("b2", r.b2r.at[g, v], 4 * g + v, at_y(v))
        r.zs[g, 2:4] = four(r.b2r.at[g]).astype(BF)

        @pl.loop(0, 4)
        def _(i):
            @pl.when(8 * g + 2 * i + p != z)
            def _():
                z_copy(g, i).start()

    home(1, 2, 1, half)

    g = r.gn[1]
    r.gx[...] = g.astype(BF).reshape(2, 4, 16, 768)
    for d in range(1, 4):
        v = (y + d) % 4
        go("gx", r.gx.at[:, v], r.xg.at[pl.ds(2 * y, 2)], d, y, at_y(v))
    r.xg[pl.ds(2 * y, 2)] = r.gx[:, y]
    g4 = r.gn[2].reshape(2, 8, 8, 768)
    r.gz[...] = jnp.concatenate([g4[0], g4[1]], axis=1).astype(BF)
    for d in range(1, 8):
        v = (k + d) % 8
        go("gz", r.gz.at[v], r.zg.at[k], d, k, at_k(v))
    r.zg[k] = r.gz[k]

    parts = [r.gn[0] * r.nrm[0] + r.gn[1] * r.nrm[1] + r.gn[2] * r.nrm[2], r.gn[0] + r.gn[1] + r.gn[2]]
    r.nk[k] = jnp.concatenate([jnp.sum(e, axis=0, keepdims=True) for e in parts], axis=0)
    for d in range(1, 8):
        go("nk", r.nk.at[k], r.nk.at[k], d, k, at_k((k + d) % 8))

    to_other_core(0)
    to_other_core(1)
    own_part(0)
    sum_first(0)
    own_part(1)

    for d in range(1, 8):
        v = (k + d) % 8
        arrived("nk", r.nk.at[v], v, at_k(v))
    both = r.nk[0]
    for v in range(1, 8):
        both = both + r.nk[v]
    r.ny[y] = jnp.where(core == 0, both[0:1], both[1:2])
    for d in range(1, 4):
        go("ny", r.ny.at[y], r.ny.at[y], d, y, at_y((y + d) % 4))

    for d in range(1, 4):
        v = (y + d) % 4
        arrived("gx", r.xg.at[pl.ds(2 * v, 2)], v, at_y(v))
    for d in range(1, 8):
        v = (k + d) % 8
        arrived("gz", r.zg.at[v], v, at_k(v))
    perm_g = one_hot(128, 128, lambda i: (i % 16) * 8 + i // 16)
    total = dot(perm_g, r.zg[...].reshape(128, 768)) + r.xg[...].reshape(128, 768).astype(F32)
    r.rb[...] = fold(total.reshape(16, 8, 768)).astype(BF).reshape(8, 2, 16, 384)

    def return_sends(i):
        @pl.loop(1 + 5 * i, 6 + 5 * i)
        def _(d):
            c = (z + d) % 16
            rcopy("rt", r.rb.at[c % 8, c // 8], r.ret.at[z], d, z, at_z(c)).start()

    sum_first(1, return_sends)
    for d in range(1, 4):
        v = (y + d) % 4
        arrived("ny", r.ny.at[v], v, at_y(v))
    r.nz[z] = (r.ny[0] + r.ny[1]) + (r.ny[2] + r.ny[3])

    r.ret[z] = r.rb[z_lo, z_hi]

    @pl.loop(1, 16)
    def _(d):
        rcopy("nz", r.nz.at[z], r.nz.at[z], d, z, at_z((z + d) % 16)).start()

    sum_second(0)
    sum_second(1)

    sum_third(0)
    sum_third(1)

    @pl.when(holder)
    def _():
        r.zr[z] = r.zs[z_hi, z_lo // 2]

    @pl.loop(1, 16)
    def _(d):
        c = (z + d) % 16
        arrived("rt", r.ret.at[c], c, at_z(c))

    scaled = (r.gn[0] + unfold(r.ret[...])) * gain_row
    nrm = r.nrm[0]
    m1 = jnp.mean(scaled, axis=-1, keepdims=True)
    m2 = jnp.mean(scaled * nrm, axis=-1, keepdims=True)
    c_rows = r.c16[0].astype(F32)
    rows = (c_rows + r.inv_y[:, :1] * (scaled - m1 - nrm * m2)).astype(BF)
    perm_b = one_hot(128, 128, lambda i: (i % 16) * 8 + i // 16)
    r.tok_out[...] = dot(perm_b, rows).astype(BF)
    store_tok = pltpu.make_async_copy(r.tok_out, tok_res, lsem.at[5])
    store_tok.start()

    @pl.loop(1, 16)
    def _(d):
        c = (z + d) % 16
        arrived("nz", r.nz.at[c], c, at_z(c))

    row = r.nz[0]
    for c in range(1, 16):
        row = row + r.nz[c]
    r.norm_out[core] = row
    go("no", r.norm_out.at[core], r.norm_out.at[core], 0, core, pair)

    def final_copies():
        return [rcopy("f", r.qr.at[core], r.qr.at[core], d, core, quad(d)[1]) for d in range(1, 4)]

    @pl.when(holder)
    def _():
        @pl.loop(1, 16)
        def _(d):
            c = (z + d) % 16
            arrived("z", r.zr.at[c], c, at_z(c))

        z_total = r.zr[0].astype(F32)
        for c in range(1, 16):
            z_total = z_total + r.zr[c].astype(F32)
        r.qr[core] = z_total
        for copy in final_copies():
            copy.start()
        arrived("f", r.qr.at[1 - core], 1 - core, pair)

    @pl.when(jnp.logical_not(holder))
    def _():
        for d in range(2):
            arrived("f", r.qr.at[d], d, at_k((x + 1 - 2 * p) * 2 + d))

    arrived("no", r.norm_out.at[1 - core], 1 - core, pair)
    store_norm = pltpu.make_async_copy(r.norm_out, norm_res, lsem.at[6])
    store_norm.start()
    store_w = pltpu.make_async_copy(r.qr, w_res, lsem.at[7])
    store_w.start()

    for copy in sends:
        copy.wait_send()

    @pl.loop(1, 16)
    def _(d):
        c = (z + d) % 16
        dev = at_z(c)
        for e in range(2):
            token_copy(e, d).wait_send()
        rcopy("rt", r.rb.at[c % 8, c // 8], r.ret.at[z], d, z, dev).wait_send()
        rcopy("nz", r.nz.at[z], r.nz.at[z], d, z, dev).wait_send()

    for g in range(2):
        @pl.loop(0, 4)
        def _(i):
            @pl.when(8 * g + 2 * i + p != z)
            def _():
                z_copy(g, i).wait_send()

    @pl.when(holder)
    def _():
        @pl.loop(1, 16)
        def _(d):
            rcopy("wz", r.wpart.at[core], w_mine, d, z, at_z((z + d) % 16)).wait_send()

        for copy in final_copies():
            copy.wait_send()

    store_tok.wait()
    store_norm.wait()
    store_w.wait()


def per_device(tokens, cotangent, weights, norm_gain, norm_bias):
    scratch = list(BUFFERS.values())
    for count in SEMAPHORES.values():
        scratch += [pltpu.SemaphoreType.DMA((count,))] * 2
    scratch.append(pltpu.SemaphoreType.DMA((8,)))
    anywhere = pl.BlockSpec(memory_space=pltpu.HBM)
    grad_tok, grad_w, grad_norm = pl.pallas_call(
        kernel,
        out_shape=(
            jax.ShapeDtypeStruct((128, 768), BF),
            jax.ShapeDtypeStruct((2, 48, 128), F32),
            jax.ShapeDtypeStruct((2, 1, 768), F32),
        ),
        in_specs=[anywhere] * 5,
        out_specs=(anywhere,) * 3,
        scratch_shapes=scratch,
        compiler_params=pltpu.CompilerParams(
            collective_id=0, has_side_effects=True, vmem_limit_bytes=60 * 1024 * 1024
        ),
        name="axial_backward",
    )(tokens.reshape(128, 768), cotangent.reshape(128, 768), weights, norm_gain, norm_bias)
    member = lax.axis_index("slab") % 4
    mine = lax.dynamic_slice(grad_w, (0, member * 12, 0), (2, 12, 128))
    mine = mine.reshape(2, 12, 2, 64).transpose(1, 0, 2, 3).reshape(12, 4, 64)
    return grad_tok.reshape(tokens.shape), mine, grad_norm.reshape(2, 768)


def solution(mesh):
    return jax.shard_map(
        per_device,
        mesh=mesh,
        in_specs=(
            P("slab", "head", None, None),
            P("slab", "head", None, None),
            P("slab", None, "head"),
            P(),
            P(),
        ),
        out_specs=(P("slab", "head", None, None), P("slab", None, "head"), P()),
        check_vma=False,
    )
```

time: 105 us -> 95.2 us (0.907)
  Pallas kernels: 98.9 us -> 88.3 us
    pallas_call x1, Pallas kernels: 98.9 us -> 88.3 us  [per_device(): pl.pallas_call(kernel, out_shape=(jax.ShapeDtypeStruct((128, 768), BF), j...]
    unnamed x12 -> x4, local copies, waits for them, and re-layouts: 3.81 us -> 2.9 us
where the time goes in v3:
time: 95.2 us; the launch traced here: 93.4 us
  Pallas kernels  88.3 us (93%)
  local copies, waits for them, and re-layouts  4.37 us (5%)
    pallas_call x1, Pallas kernels, per_device(): pl.pallas_call(kernel, out_shape=(jax.ShapeDtypeStruct((128, 768), BF), j...  88.3 us
    unnamed x4, local copies, waits for them, and re-layouts  2.9 us

profile of v3, /device:TPU:1, one launch (start us, length us, event | category | flops | bytes accessed | tf_op | source)
XLA Modules:
  0.0 93.4 jit_solution(1832511704350754714)
XLA Ops:
  0.6 88.3 %axial_backward.1 = (bf16[128,768]{1,0:T(8,128)(2,1)}, f32[2,48,128]{2,1,0:T(8,128)}, f32[2,1,768]{2,1,0:T(1,128)}) custom-call(bf16[128,768]{1,0:T(8,128)(2,1)} %bitcast.11, bf16[128,768]{1,0:T(8,128)(2,1)} %bitcast.12, bf16[12,4,64]{2,1,0:T(4,128)(2,1)} %w_in.1, f32[768]{0:T(1024)} %gain_in.1, f32[768]{0:T(1024)} %bias_in.1), custom_call_target="tpu_custom_call" | custom-call | tf_op jit(solution)/shard_map/axial_backward/pallas_call | solution.py:661
  89.0 0.8 constant_dynamic-slice_fusion
  89.8 0.7 reshape.27
  90.5 0.0 copy-start
  90.5 0.7 copy-done
  91.1 0.6 copy.11
  91.7 1.6 %copy.13 = bf16[1,8,16,768]{3,2,1,0:T(8,128)(2,1)} copy(bf16[1,8,16,768]{3,2,1,0:T(8,128)(2,1)} %bitcast.13) | data formatting | bytes 393216
  (1 shorter events, 0.0 us)
Async XLA Ops:
  90.5 0.7 copy-start

commit v4 on v3

--- a/solution.py
+++ b/solution.py
@@ -206,6 +206,8 @@
         def _(i):
             token_copy(e, 8 + (1 - 2 * (i % 2)) * ((i + 1) // 2)).start()
 
+    token_sends(0, 0, 3)
+
     gain_row, bias_row = r.gain[...].reshape(1, 768), r.bias[...].reshape(1, 768)
 
     def prepare_cotangent(idx, rows):
@@ -264,7 +266,7 @@
     for d in range(1, 4):
         go("wa1", w_a(x), w_a(x), d, x, at_x((x + d) % 4))
         go("wb1", w_b(y), w_b(y), d, y, at_y((y + d) % 4))
-    token_sends(0, 0, 8)
+    token_sends(0, 3, 8)
     for e in range(2):
         r.p1[e, z_lo, z_hi] = r.send_rows[e, z]
 
@@ -541,7 +543,9 @@
             c = (z + d) % 16
             rcopy("rt", r.rb.at[c % 8, c // 8], r.ret.at[z], d, z, at_z(c)).start()
 
-    sum_first(1, return_sends)
+    for i in range(3):
+        return_sends(i)
+    sum_first(1)
     for d in range(1, 4):
         v = (y + d) % 4
         arrived("ny", r.ny.at[v], v, at_y(v))

time: 95.2 us -> 93.9 us (0.986)
  no operation moved by 1% of the time
where the time goes in v4:
time: 93.9 us; the launch traced here: 92.9 us
  Pallas kernels  87.9 us (94%)
  local copies, waits for them, and re-layouts  4.37 us (5%)
    pallas_call x1, Pallas kernels, per_device(): pl.pallas_call(kernel, out_shape=(jax.ShapeDtypeStruct((128, 768), BF), j...  87.9 us
    unnamed x4, local copies, waits for them, and re-layouts  2.9 us

profile of v4, /device:TPU:1, one launch (start us, length us, event | category | flops | bytes accessed | tf_op | source)
XLA Modules:
  0.0 92.9 jit_solution(668195931391524138)
XLA Ops:
  0.6 87.9 %axial_backward.1 = (bf16[128,768]{1,0:T(8,128)(2,1)}, f32[2,48,128]{2,1,0:T(8,128)}, f32[2,1,768]{2,1,0:T(1,128)}) custom-call(bf16[128,768]{1,0:T(8,128)(2,1)} %bitcast.11, bf16[128,768]{1,0:T(8,128)(2,1)} %bitcast.12, bf16[12,4,64]{2,1,0:T(4,128)(2,1)} %w_in.1, f32[768]{0:T(1024)} %gain_in.1, f32[768]{0:T(1024)} %bias_in.1), custom_call_target="tpu_custom_call" | custom-call | tf_op jit(solution)/shard_map/axial_backward/pallas_call | solution.py:665
  88.5 0.8 constant_dynamic-slice_fusion
  89.3 0.7 reshape.27
  90.0 0.0 copy-start
  90.0 0.7 copy-done
  90.7 0.6 copy.11
  91.3 1.6 %copy.13 = bf16[1,8,16,768]{3,2,1,0:T(8,128)(2,1)} copy(bf16[1,8,16,768]{3,2,1,0:T(8,128)(2,1)} %bitcast.13) | data formatting | bytes 393216
  (1 shorter events, 0.0 us)
Async XLA Ops:
  90.0 0.7 copy-start

commit v5 on v4

--- a/solution.py
+++ b/solution.py
@@ -90,6 +90,10 @@
     return lax.dot_general(a, b, (((0,), (0,)), ((), ())), preferred_element_type=F32)
 
 
+def both_ways(i):
+    return 8 + (1 - 2 * (i % 2)) * ((i + 1) // 2)
+
+
 def fold(a):
     return jnp.concatenate([a[:, :, :384], a[:, :, 384:]], axis=1)
 
@@ -204,7 +208,7 @@
     def token_sends(e, start, stop):
         @pl.loop(start, stop)
         def _(i):
-            token_copy(e, 8 + (1 - 2 * (i % 2)) * ((i + 1) // 2)).start()
+            token_copy(e, both_ways(i)).start()
 
     token_sends(0, 0, 3)
 
@@ -242,8 +246,9 @@
     def _():
         w_mine[...] = r.wpart[core]
 
-        @pl.loop(1, 16)
-        def _(d):
+        @pl.loop(0, 15)
+        def _(i):
+            d = both_ways(i)
             rcopy("wz", r.wpart.at[core], w_mine, d, z, at_z((z + d) % 16)).start()
 
     r.inv_y[...] = jnp.broadcast_to(prepare(0, r.send_rows[0]), (128, 128))
@@ -325,7 +330,16 @@
         theirs = r.wb.at[core, 1, :, :, j_of(v)]
         arrived("wb2", theirs, v, at_x(v))
         go("wcb", theirs, theirs, d, v, pair)
+    def separate(part):
+        @pl.loop(0, 2)
+        def _(g):
+            for e in range(2):
+                both = [r.wb[part, g, 2 * e + h].reshape(768, 128).astype(F32) for h in range(2)]
+                for h, block in enumerate(swap(*both)):
+                    r.wsep[2 * part + h, g, :, e * 128:(e + 1) * 128] = block.astype(BF)
+
     second_hop(1)
+    separate(core)
 
     for d in range(4):
         v = (y + d) % 4
@@ -333,16 +347,10 @@
         v = (x + d) % 4
         arrived("wcb", r.wb.at[1 - core, 1, :, :, j_of(v)], v, pair)
 
+    separate(1 - core)
+
     row_i = lax.broadcasted_iota(jnp.int32, (128, 128), 0)
     col_i = lax.broadcasted_iota(jnp.int32, (128, 128), 1)
-
-    @pl.loop(0, 4)
-    def _(i):
-        part, g = i // 2, i % 2
-        for e in range(2):
-            both = [r.wb[part, g, 2 * e + h].reshape(768, 128).astype(F32) for h in range(2)]
-            for h, block in enumerate(swap(*both)):
-                r.wsep[2 * part + h, g, :, e * 128:(e + 1) * 128] = block.astype(BF)
 
     def lines(q, kk, v, u, same):
         lane_head = lax.broadcasted_iota(jnp.int32, (128, 256), 1) // 64
@@ -538,8 +546,9 @@
     r.rb[...] = fold(total.reshape(16, 8, 768)).astype(BF).reshape(8, 2, 16, 384)
 
     def return_sends(i):
-        @pl.loop(1 + 5 * i, 6 + 5 * i)
-        def _(d):
+        @pl.loop(5 * i, 5 * i + 5)
+        def _(n):
+            d = both_ways(n)
             c = (z + d) % 16
             rcopy("rt", r.rb.at[c % 8, c // 8], r.ret.at[z], d, z, at_z(c)).start()
 
@@ -553,8 +562,9 @@
 
     r.ret[z] = r.rb[z_lo, z_hi]
 
-    @pl.loop(1, 16)
-    def _(d):
+    @pl.loop(0, 15)
+    def _(i):
+        d = both_ways(i)
         rcopy("nz", r.nz.at[z], r.nz.at[z], d, z, at_z((z + d) % 16)).start()
 
     sum_second(0)

time: 93.9 us -> 93.2 us (level)
  the two profiles are of different devices: /device:TPU:1 before, /device:TPU:33 now
where the time goes in v5:
time: 93.2 us; the launch traced here: 92.9 us
  Pallas kernels  87.9 us (94%)
  local copies, waits for them, and re-layouts  4.37 us (5%)
    pallas_call x1, Pallas kernels, per_device(): pl.pallas_call(kernel, out_shape=(jax.ShapeDtypeStruct((128, 768), BF), j...  87.9 us
    unnamed x4, local copies, waits for them, and re-layouts  2.9 us

profile of v5, /device:TPU:33, one launch (start us, length us, event | category | flops | bytes accessed | tf_op | source)
XLA Modules:
  0.0 92.9 jit_solution(2393731757487359929)
XLA Ops:
  0.6 87.9 %axial_backward.1 = (bf16[128,768]{1,0:T(8,128)(2,1)}, f32[2,48,128]{2,1,0:T(8,128)}, f32[2,1,768]{2,1,0:T(1,128)}) custom-call(bf16[128,768]{1,0:T(8,128)(2,1)} %bitcast.11, bf16[128,768]{1,0:T(8,128)(2,1)} %bitcast.12, bf16[12,4,64]{2,1,0:T(4,128)(2,1)} %w_in.1, f32[768]{0:T(1024)} %gain_in.1, f32[768]{0:T(1024)} %bias_in.1), custom_call_target="tpu_custom_call" | custom-call | tf_op jit(solution)/shard_map/axial_backward/pallas_call | solution.py:675
  88.5 0.8 constant_dynamic-slice_fusion
  89.3 0.7 reshape.27
  90.0 0.0 copy-start
  90.0 0.7 copy-done
  90.7 0.6 copy.11
  91.3 1.6 %copy.13 = bf16[1,8,16,768]{3,2,1,0:T(8,128)(2,1)} copy(bf16[1,8,16,768]{3,2,1,0:T(8,128)(2,1)} %bitcast.13) | data formatting | bytes 393216
  (1 shorter events, 0.0 us)
Async XLA Ops:
  90.0 0.7 copy-start

commit v6 on v5

--- a/solution.py
+++ b/solution.py
@@ -65,7 +65,7 @@
     "nz": VM((16, 1, 768), F32),
 }
 SEMAPHORES = {
-    "q": 4, "wz": 16, "wa1": 4, "wb1": 4, "wa2": 4, "wb2": 4, "wca": 4, "wcb": 4,
+    "q": 4, "wz": 16, "wa1": 4, "wb1": 4, "wa2": 8, "wb2": 8, "wca": 8, "wcb": 8,
     "p1": 32, "xl": 8, "zl": 16, "gx": 4, "gz": 8, "rt": 16,
     "c": 2, "a1": 8, "b1": 8, "a2": 8, "b2": 8, "z": 16, "f": 4,
     "nk": 8, "ny": 4, "nz": 16, "no": 2,
@@ -278,17 +278,31 @@
     for d in range(1, 4):
         v = (x + d) % 4
         arrived("wa1", w_a(v), v, at_x(v))
-    a_mine, b_mine = r.wb.at[core, 0, y], r.wb.at[core, 1, :, :, j]
-    go("wca", a_mine, a_mine, 0, y, pair)
+    def half_a(of, v, h):
+        return r.wb.at[of, 0, v, 2 * h:2 * h + 2]
+
+    def half_b(of, v, h):
+        return r.wb.at[of, 1, 2 * h:2 * h + 2, :, j_of(v)]
+
+    def halves(name, half, v, d, dev):
+        for h in range(2):
+            go(name, half(core, v, h), half(core, v, h), 2 * d + h, 2 * v + h, dev)
+
+    def hand_on(name, across, half, v, d, dev):
+        for h in range(2):
+            arrived(name, half(core, v, h), 2 * v + h, dev)
+            go(across, half(core, v, h), half(core, v, h), 2 * d + h, 2 * v + h, pair)
+
+    halves("wca", half_a, y, 0, pair)
     for d, span in ((1, (8, 10)), (3, (10, 12)), (2, (12, 15))):
-        go("wa2", a_mine, a_mine, d, y, at_y((y + d) % 4))
+        halves("wa2", half_a, y, d, at_y((y + d) % 4))
         token_sends(0, *span)
     for d in range(1, 4):
         v = (y + d) % 4
         arrived("wb1", w_b(v), v, at_y(v))
-    go("wcb", b_mine, b_mine, 0, x, pair)
+    halves("wcb", half_b, x, 0, pair)
     for d, span in ((1, (0, 4)), (3, (4, 8)), (2, (8, 15))):
-        go("wb2", b_mine, b_mine, d, x, at_x((x + d) % 4))
+        halves("wb2", half_b, x, d, at_x((x + d) % 4))
         token_sends(1, *span)
 
     perm_v = one_hot(
@@ -323,13 +337,9 @@
 
     for d in (1, 3, 2):
         v = (y + d) % 4
-        theirs = r.wb.at[core, 0, v]
-        arrived("wa2", theirs, v, at_y(v))
-        go("wca", theirs, theirs, d, v, pair)
+        hand_on("wa2", "wca", half_a, v, d, at_y(v))
         v = (x + d) % 4
-        theirs = r.wb.at[core, 1, :, :, j_of(v)]
-        arrived("wb2", theirs, v, at_x(v))
-        go("wcb", theirs, theirs, d, v, pair)
+        hand_on("wb2", "wcb", half_b, v, d, at_x(v))
     def separate(part):
         @pl.loop(0, 2)
         def _(g):
@@ -343,9 +353,11 @@
 
     for d in range(4):
         v = (y + d) % 4
-        arrived("wca", r.wb.at[1 - core, 0, v], v, pair)
+        for h in range(2):
+            arrived("wca", half_a(1 - core, v, h), 2 * v + h, pair)
         v = (x + d) % 4
-        arrived("wcb", r.wb.at[1 - core, 1, :, :, j_of(v)], v, pair)
+        for h in range(2):
+            arrived("wcb", half_b(1 - core, v, h), 2 * v + h, pair)
 
     separate(1 - core)
 

time: 93.2 us -> 93.5 us (level)
  no operation moved by 1% of the time
where the time goes in v6:
time: 93.5 us; the launch traced here: 93.3 us
  Pallas kernels  88.2 us (94%)
  local copies, waits for them, and re-layouts  4.37 us (5%)
    pallas_call x1, Pallas kernels, per_device(): pl.pallas_call(kernel, out_shape=(jax.ShapeDtypeStruct((128, 768), BF), j...  88.2 us
    unnamed x4, local copies, waits for them, and re-layouts  2.9 us

profile of v6, /device:TPU:33, one launch (start us, length us, event | category | flops | bytes accessed | tf_op | source)
XLA Modules:
  0.0 93.3 jit_solution(9941627511626197704)
XLA Ops:
  0.6 88.2 %axial_backward.1 = (bf16[128,768]{1,0:T(8,128)(2,1)}, f32[2,48,128]{2,1,0:T(8,128)}, f32[2,1,768]{2,1,0:T(1,128)}) custom-call(bf16[128,768]{1,0:T(8,128)(2,1)} %bitcast.11, bf16[128,768]{1,0:T(8,128)(2,1)} %bitcast.12, bf16[12,4,64]{2,1,0:T(4,128)(2,1)} %w_in.1, f32[768]{0:T(1024)} %gain_in.1, f32[768]{0:T(1024)} %bias_in.1), custom_call_target="tpu_custom_call" | custom-call | tf_op jit(solution)/shard_map/axial_backward/pallas_call | solution.py:687
  88.9 0.8 constant_dynamic-slice_fusion
  89.7 0.7 reshape.27
  90.4 0.0 copy-start
  90.4 0.7 copy-done
  91.1 0.6 copy.11
  91.7 1.6 %copy.13 = bf16[1,8,16,768]{3,2,1,0:T(8,128)(2,1)} copy(bf16[1,8,16,768]{3,2,1,0:T(8,128)(2,1)} %bitcast.13) | data formatting | bytes 393216
  (1 shorter events, 0.0 us)
Async XLA Ops:
  90.4 0.7 copy-start
